TPU v7x, 512 devices: a whole 4x4x16 slice. The times are simulated.
512 devices in a mesh: dp: 64 (over z, y_hi, core), tensor: 8 (over x, y_lo).
Axes of the slice: x: 4, y: 4 (y_hi: 2, y_lo: 2; y = y_hi * 2 + y_lo), z: 16, core: 2. Of those that a mesh axis runs over, the one named last changes fastest.
Arguments:
- text_hidden: bfloat16 [10240, 1152], P('dp'), may hold values from -6 to 6
- ln_gain: float32 [1152], replicated, may hold values from 0.25 to 1.75
- up_weight: bfloat16 [1152, 4304], P(None, 'tensor'), may hold values from -0.1875 to 0.1875
- down_weight: bfloat16 [4304, 1152], P('tensor'), may hold values from -0.09375 to 0.09375
- final_gain: float32 [1152], replicated, may hold values from 0.1 to 1.9
- head_weight: bfloat16 [1152, 1152], P('tensor'), may hold values from -0.1875 to 0.1875
- image_features: bfloat16 [10240, 1152], P('dp'), may hold values from -16 to 16
- vision_weight: bfloat16 [1152, 1152], P(None, 'tensor'), may hold values from -0.1875 to 0.1875
Outputs:
- text_grad: float32 [10240, 1152], P(('dp', 'tensor'))
- vision_grad: float32 [1152, 1152], P('dp', 'tensor')
All inputs are finite; a program needn't handle non-finite values.
Results may differ from a plain program's by a relative error of at most 0.0065.
Values may be sent and summed in bfloat16 or wider, within the bound.
A program may use at most 64 MiB of HBM per device.

v0:
```python
import jax
import jax.numpy as jnp
from jax import lax
from jax.sharding import PartitionSpec as P

logit_scale = 100.0
logit_bias = -4.0
norm_eps = 1e-06


def from_behind(block, axis, distance):
    devices = range(lax.axis_size(axis))
    route = [((i - distance) % len(devices), i) for i in devices]
    return lax.ppermute(block, axis, route)


def contract(left_side, right_side, left_dim, right_dim):
    return lax.dot_general(
        left_side,
        right_side,
        (((left_dim,), (right_dim,)), ((), ())),
        preferred_element_type=jnp.float32,
    )


def layer_norm(values, gain_row):
    center = values - jnp.mean(values, axis=1, keepdims=True)
    spread = jnp.mean(center * center, axis=1, keepdims=True)
    return center * lax.rsqrt(spread + norm_eps) * gain_row


def unit_rows(values):
    inverse = lax.rsqrt(jnp.sum(values * values, axis=1, keepdims=True) + norm_eps)
    return (values * inverse, inverse)


def tile_terms(image_unit, text_block, positive, image_rows):
    logits = logit_scale * contract(image_unit, text_block, 1, 1) + logit_bias
    weights = ((jax.nn.sigmoid(logits) - positive) * (logit_scale / image_rows)).astype(
        jnp.bfloat16
    )
    return (weights, contract(weights, image_unit, 0, 0))


def repeat_visits(visits, visit_block, carried):

    def two_visits(turn_index, inner):
        return visit_block(2 * turn_index + 1, visit_block(2 * turn_index, inner))

    carried = lax.fori_loop(0, visits // 2, two_visits, carried)
    carried = visit_block(visits - 1, carried)
    return carried


def local(
    text_hidden,
    ln_gain,
    up_weight,
    down_weight,
    final_gain,
    head_weight,
    image_features,
    vision_weight,
):
    tensor_rank = lax.axis_index("tensor")
    tensor_size = lax.axis_size("tensor")
    image_rows = text_hidden.shape[0]
    text_rows = image_rows // tensor_size
    head_rows = head_weight.shape[0]
    hidden = text_hidden.astype(jnp.float32)
    lifted = layer_norm(hidden, ln_gain).astype(jnp.bfloat16)
    active = jax.nn.gelu(
        jnp.dot(lifted, up_weight, preferred_element_type=jnp.float32), approximate=True
    ).astype(jnp.bfloat16)
    mixed_sum = lax.psum(jnp.dot(active, down_weight, preferred_element_type=jnp.float32), "tensor")
    normed = layer_norm(hidden + mixed_sum, final_gain).astype(jnp.bfloat16)
    feature_cols = lax.dynamic_slice_in_dim(normed, tensor_rank * head_rows, head_rows, 1)
    head_part = jnp.dot(feature_cols, head_weight, preferred_element_type=jnp.float32)
    head_total = lax.psum(head_part, "tensor")
    text_emb = lax.dynamic_slice_in_dim(head_total, tensor_rank * text_rows, text_rows, 0)
    text_unit = unit_rows(text_emb)[0].astype(jnp.bfloat16)
    image_part = jnp.dot(image_features, vision_weight, preferred_element_type=jnp.float32)
    image_emb = lax.all_gather(image_part, "tensor", axis=1, tiled=True)
    image_float, inverse = unit_rows(image_emb)
    image_unit = image_float.astype(jnp.bfloat16)
    embed_width = image_unit.shape[1]
    data_size = lax.axis_size("dp")
    row_ids = lax.broadcasted_iota(jnp.int32, (image_rows, text_rows), 0)
    col_ids = lax.broadcasted_iota(jnp.int32, (image_rows, text_rows), 1)
    diagonal = (row_ids == tensor_rank * text_rows + col_ids).astype(jnp.float32)
    own_weights, own_term = tile_terms(image_unit, text_unit, diagonal, image_rows)
    coef_store = jnp.zeros((image_rows, data_size * text_rows), jnp.bfloat16)
    block_store = jnp.zeros((data_size * text_rows, embed_width), jnp.bfloat16)
    coef_store = lax.dynamic_update_slice_in_dim(coef_store, own_weights, 0, 1)
    block_store = lax.dynamic_update_slice_in_dim(block_store, text_unit, 0, 0)

    def make_visit(move_block, move_grads, first_slot):

        def visit_block(position, carried):
            text_block, grad_block, coefs, blocks = carried
            text_block = move_block(text_block)
            grad_block = move_grads(grad_block)
            weights, text_term = tile_terms(image_unit, text_block, 0.0, image_rows)
            offset = (first_slot + position) * text_rows
            coefs = lax.dynamic_update_slice_in_dim(coefs, weights, offset, 1)
            blocks = lax.dynamic_update_slice_in_dim(blocks, text_block, offset, 0)
            return (text_block, grad_block + text_term, coefs, blocks)

        return visit_block

    def pass_block(text_block):
        return from_behind(text_block, "dp", 1)

    def pass_grads(grad_block):
        return from_behind(grad_block, "dp", 1)

    carried = repeat_visits(
        data_size - 1,
        make_visit(pass_block, pass_grads, 1),
        (text_unit, own_term, coef_store, block_store),
    )
    text_grad = pass_grads(carried[1])
    coef_store, block_store = (carried[2], carried[3])
    image_grad = jnp.dot(coef_store, block_store, preferred_element_type=jnp.float32)
    radial = jnp.sum(image_float * image_grad, axis=1, keepdims=True)
    emb_grad = (image_grad - image_float * radial) * inverse
    column_grad = lax.psum_scatter(emb_grad, "tensor", scatter_dimension=1, tiled=True).astype(
        jnp.bfloat16
    )
    weight_part = contract(image_features, column_grad, 0, 0)
    vision_grad = lax.psum_scatter(weight_part, "dp", scatter_dimension=0, tiled=True)
    return (text_grad, vision_grad)


def solution(mesh):
    placed = (
        P("dp", None),
        P(),
        P(None, "tensor"),
        P("tensor", None),
        P(),
        P("tensor", None),
        P("dp", None),
        P(None, "tensor"),
    )
    return jax.shard_map(
        local,
        mesh=mesh,
        in_specs=placed,
        out_specs=(P(("dp", "tensor"), None), P("dp", "tensor")),
        check_vma=False,
    )
```

profile of v0, /device:TPU:1, one launch (start us, length us, event | category | flops | bytes accessed | tf_op | source)
XLA Modules:
  0.0 1647.4 jit_solution(6380371158220498561)
XLA Ops:
  9.7 3.5 fusion.49
  14.4 32.9 %all_gather.3 = f32[160,1152]{0,1:T(8,128)S(1)} all-gather(f32[160,144]{0,1:T(8,128)S(1)} %fusion.75), channel_id=1, replica_groups=mesh['dp'=64,'tensor'=8] {'tensor'}, dimensions={1}, use_global_device_ids=true | all-gather | bytes 829440 | tf_op jit(solution)/shard_map/all_gather | solution.py:83
  47.4 62.6 %all-reduce.7.cloned.1.call-done = f32[160,1152]{1,0:T(8,128)} async-done(((f32[160,1152]{1,0:T(8,128)}), f32[160,1152]{1,0:T(8,128)}) %all-reduce.7.cloned.1.call-update) | async-done | bytes 737296 | tf_op jit(solution)/shard_map/psum | solution.py:75
  114.1 90.4 %all-reduce.9.cloned.1.call-done = f32[160,1152]{1,0:T(8,128)} async-done(((f32[160,1152]{1,0:T(8,128)}), f32[160,1152]{1,0:T(8,128)}) %all-reduce.9.cloned.1.call-update) | async-done | bytes 737296 | tf_op jit(solution)/shard_map/psum | solution.py:79
  212.6 857.9 %while.21 = (s32[]{:T(128)}, bf16[20,1152]{1,0:T(8,128)(2,1)}, f32[20,1152]{1,0:T(8,128)}, bf16[160,1280]{0,1:T(8,128)(2,1)}, bf16[1280,1152]{1,0:T(8,128)(2,1)}...) while((s32[]{:T(128)}, bf16[20,1152]{1,0:T(8,128)(2,1)}, ...), condition=%wide.region_9.0_spmd, body=%wide.region_8.0_spmd.sunk | while | flops 29582080 | bytes 3461533 | solution.py:50
  212.6 9.7 collective-permute-start
  226.7 5.3 collective-permute-start.1
  242.1 4.9 collective-permute-start
  251.4 5.3 collective-permute-start.1
  266.8 5.5 collective-permute-start
  294.3 3.3 collective-permute-start
  299.6 4.7 collective-permute-done
  312.9 3.2 collective-permute-done.1
  325.9 6.0 collective-permute-done
  340.6 3.2 collective-permute-done.1
  353.6 6.0 collective-permute-done
  381.4 6.0 collective-permute-done
  396.1 3.2 collective-permute-done.1
  409.1 6.0 collective-permute-done
  436.8 6.0 collective-permute-done
  451.5 3.2 collective-permute-done.1
  464.5 6.0 collective-permute-done
  479.2 3.2 collective-permute-done.1
  492.2 6.0 collective-permute-done
  507.0 3.2 collective-permute-done.1
  519.9 6.0 collective-permute-done
  534.7 3.2 collective-permute-done.1
  547.7 6.0 collective-permute-done
  562.4 3.2 collective-permute-done.1
  575.4 6.0 collective-permute-done
  590.1 3.2 collective-permute-done.1
  603.1 6.0 collective-permute-done
  617.9 3.2 collective-permute-done.1
  630.8 6.0 collective-permute-done
  645.6 3.2 collective-permute-done.1
  658.5 6.0 collective-permute-done
  673.3 3.2 collective-permute-done.1
  686.3 6.0 collective-permute-done
  701.0 3.2 collective-permute-done.1
  714.0 6.0 collective-permute-done
  741.7 6.0 collective-permute-done
  756.5 3.2 collective-permute-done.1
  769.4 6.0 collective-permute-done
  784.2 3.2 collective-permute-done.1
  797.1 6.0 collective-permute-done
  824.9 6.0 collective-permute-done
  852.6 6.0 collective-permute-done
  867.3 3.2 collective-permute-done.1
  880.3 6.0 collective-permute-done
  895.1 3.2 collective-permute-done.1
  908.0 6.0 collective-permute-done
  935.8 6.0 collective-permute-done
  950.5 3.2 collective-permute-done.1
  963.5 6.0 collective-permute-done
  991.2 6.0 collective-permute-done
  1018.9 6.0 collective-permute-done
  1046.7 6.0 collective-permute-done
  1061.4 3.2 collective-permute-done.1
  1072.4 7.9 collective-permute-done.5
  1083.3 3.4 multiply_reduce_fusion
  1088.0 47.0 %reduce-scatter.3.cloned.1.call-done = f32[160,144]{0,1:T(8,128)} async-done(((f32[160,1152]{0,1:T(8,128)}), f32[160,144]{0,1:T(8,128)}) %reduce-scatter.3.cloned.1.call-update) | async-done | bytes 92176 | tf_op jit(solution)/shard_map/reduce_scatter | solution.py:127
  1137.0 9.5 collective-permute-start.4
  1148.5 5.8 collective-permute-start.6
  1156.3 482.2 %all-reduce.11.cloned.1.call-done = f32[1152,144]{0,1:T(8,128)} async-done(((f32[1152,144]{0,1:T(8,128)}), f32[1152,144]{0,1:T(8,128)}) %all-reduce.11.cloned.1.call-update) | async-done | bytes 663568
  (534 shorter events, 623.5 us)
Async XLA Ops:
  7.2 102.9 %all-reduce.7.cloned.1.call-start = ((), (), s32[]{:S(2)}) async-start(), calls=%async_computation.1 | async-start | bytes 1474560 | tf_op jit(solution)/shard_map/psum | solution.py:75
  13.2 191.2 %all-reduce.9.cloned.1.call-start = ((), (), s32[]{:S(2)}) async-start(), calls=%async_computation.2 | async-start | bytes 1474560 | tf_op jit(solution)/shard_map/psum | solution.py:79
  113.6 1021.3 %reduce-scatter.3.cloned.1.call-start = ((), (), s32[]{:S(2)}) async-start(), calls=%async_computation.3 | async-start | bytes 1327104 | tf_op jit(solution)/shard_map/reduce_scatter | solution.py:127
  212.6 11.6 collective-permute-start
  222.3 11.3 collective-permute-start.2
  247.0 11.3 collective-permute-start.2
  272.3 11.3 collective-permute-start.2
  294.3 9.9 collective-permute-start
  297.6 12.6 collective-permute-start.2
  322.0 9.9 collective-permute-start
  323.9 13.9 collective-permute-start.2
  349.7 9.9 collective-permute-start
  351.7 14.0 collective-permute-start.2
  377.5 9.9 collective-permute-start
  379.4 13.9 collective-permute-start.2
  405.2 9.9 collective-permute-start
  407.1 14.0 collective-permute-start.2
  432.9 9.9 collective-permute-start
  434.8 13.9 collective-permute-start.2
  460.6 9.9 collective-permute-start
  462.6 13.9 collective-permute-start.2
  488.4 9.9 collective-permute-start
  490.3 13.9 collective-permute-start.2
  516.1 9.9 collective-permute-start
  518.0 14.0 collective-permute-start.2
  543.8 9.9 collective-permute-start
  545.7 14.0 collective-permute-start.2
  571.5 9.9 collective-permute-start
  573.4 14.0 collective-permute-start.2
  599.3 9.9 collective-permute-start
  601.2 13.9 collective-permute-start.2
  627.0 9.9 collective-permute-start
  628.9 13.9 collective-permute-start.2
  654.7 9.9 collective-permute-start
  656.6 13.9 collective-permute-start.2
  682.4 9.9 collective-permute-start
  684.3 13.9 collective-permute-start.2
  710.1 9.9 collective-permute-start
  712.0 14.0 collective-permute-start.2
  737.8 9.9 collective-permute-start
  739.8 13.9 collective-permute-start.2
  765.6 9.9 collective-permute-start
  767.5 13.9 collective-permute-start.2
  793.3 9.9 collective-permute-start
  795.2 14.0 collective-permute-start.2
  821.0 9.9 collective-permute-start
  822.9 14.0 collective-permute-start.2
  848.7 9.9 collective-permute-start
  850.7 13.9 collective-permute-start.2
  876.4 9.9 collective-permute-start
  878.4 14.0 collective-permute-start.2
  904.2 9.9 collective-permute-start
  906.1 14.0 collective-permute-start.2
  933.8 13.9 collective-permute-start.2
  959.6 9.9 collective-permute-start
  961.5 14.0 collective-permute-start.2
  987.3 9.9 collective-permute-start
  989.3 14.0 collective-permute-start.2
  1015.1 9.9 collective-permute-start
  1017.0 14.0 collective-permute-start.2
  1042.8 9.9 collective-permute-start
  1044.7 13.9 collective-permute-start.2
  1087.9 550.6 %all-reduce.11.cloned.1.call-start = ((), (), s32[]{:S(2)}) async-start(), calls=%async_computation.4 | async-start | bytes 1327104
  1137.0 11.2 collective-permute-start.4
  (75 other events, 826.7 us)
Sparse Core Ops, SparseCore 0:
  13.4 96.6 all-reduce.6
  113.7 90.7 all-reduce.8
  1088.0 46.8 reduce-scatter.2
  1137.7 500.7 all-reduce.10
where the time goes:
time: 1660 us; the launch traced here: 1650 us
  waiting for transfers between devices  959 us (58%)
  starting transfers between devices  278 us (17%)
  local copies, waits for them, and re-layouts  194 us (12%)
  matrix products  110 us (7%)
  other arithmetic  56.4 us (3%)
  blocking collectives  32.9 us (2%)
    unnamed x5, waiting for transfers between devices  482 us
    ppermute x127, starting transfers between devices, from_behind(): return lax.ppermute(block, axis, route)  278 us
    ppermute x127, waiting for transfers between devices, from_behind(): return lax.ppermute(block, axis, route)  277 us
    dot_general x129, matrix products, contract(): lax.dot_general(left_side, right_side, (((left_dim,), (right_dim,)), ((),...  102 us
    dynamic_update_slice x63, local copies, waits for them, and re-layouts, visit_block(): blocks = lax.dynamic_update_slice_in_dim(blocks, text_block, offset, 0)  98.2 us
    psum x1, waiting for transfers between devices, local(): head_total = lax.psum(head_part, 'tensor')  90.4 us
    dynamic_update_slice x63, local copies, waits for them, and re-layouts, visit_block(): coefs = lax.dynamic_update_slice_in_dim(coefs, weights, offset, 1)  86.7 us
    psum x1, waiting for transfers between devices, local(): lax.psum(jnp.dot(active, down_weight, preferred_element_type=jnp.float32)...  62.6 us
  transfers between devices with their start and end apart: 131, of which 93 were waited for; matrix products, arithmetic and copies ran while one was open for 17% of the time, Pallas kernels for 0%

commit v1 on v0

v1 whole, which is shorter than its diff:
```python
import functools

import jax
import jax.numpy as jnp
from jax import lax
from jax.experimental import pallas as pl
from jax.experimental.pallas import tpu as pltpu
from jax.sharding import PartitionSpec as P

logit_scale = 100.0
logit_bias = -4.0
norm_eps = 1e-06
MESH = pl.DeviceIdType.MESH
F32 = jnp.float32
BF16 = jnp.bfloat16

D = 1152
E = 1152
ROWS = 160
TS = 8
ZS = 16
HALF = ZS // 2
TEXTS = ROWS // TS
CHUNK = 2 * TEXTS
IMGS = 2 * ROWS
PIECE = E // (2 * TS)
COLS = E // TS
ZROWS = D // ZS


def mm(a, b):
    return jnp.dot(a, b, preferred_element_type=F32)


def layer_norm(values, gain_row):
    center = values - jnp.mean(values, axis=1, keepdims=True)
    spread = jnp.mean(center * center, axis=1, keepdims=True)
    return center * lax.rsqrt(spread + norm_eps) * gain_row


S_FEAT = 0
S_IMG = 1
S_IMGC = S_IMG + TS
S_MIX = S_IMGC + 1
S_NRM = S_MIX + TS
S_HEAD = S_NRM + TS
S_YH = S_HEAD + TS
S_AGP = S_YH + 1
S_AGM = S_AGP + HALF
S_RSP = S_AGM + HALF
S_RSM = S_RSP + HALF
S_YG = S_RSM + HALF
S_CX = S_YG + 1
S_PX = S_CX + 1
S_VRP = S_PX + TS
S_VRM = S_VRP + HALF
S_FX = S_VRM + HALF
S_ALL = S_FX + 4


def kernel(
    text_ref,
    ln_ref,
    up_ref,
    down_ref,
    fg_ref,
    head_ref,
    feat_ref,
    vis_ref,
    tg_ref,
    vg_ref,
    feats,
    part_t,
    img_s,
    img_r,
    img_f,
    img_ut,
    img_u,
    inv_ref,
    mix_s,
    mix_f,
    mix_r,
    nrm_s,
    nrm_r,
    nrm_a,
    head_s,
    head_f,
    head_r,
    yh_s,
    yh_r,
    chunk_f,
    texts,
    grads,
    eg,
    rs_s,
    rs_r,
    yg_s,
    yg_r,
    cx_s,
    cx_r,
    px_f,
    px_s,
    px_r,
    vg_all,
    vr_s,
    vr_r,
    fx,
    send_sem,
    recv_sem,
):
    d = lax.axis_index("dp")
    t = lax.axis_index("tensor")
    z = d // 4
    yh = (d // 2) % 2
    c = d % 2
    base = d - 4 * z
    z_next = (lax.rem(z + 1, ZS) * 4 + base, t)
    z_prev = (lax.rem(z + ZS - 1, ZS) * 4 + base, t)
    yh_peer = (d + 2 - 4 * yh, t)
    c_peer = (d + 1 - 2 * c, t)
    q = 2 * yh + c

    def zmod(v):
        return lax.rem(v + 2 * ZS, ZS)

    def tpeer(k):
        return lax.rem(t + k, TS)

    def rcopy(src, dst, i_send, i_recv, dev):
        return pltpu.make_async_remote_copy(
            src_ref=src,
            dst_ref=dst,
            send_sem=send_sem.at[i_send],
            recv_sem=recv_sem.at[i_recv],
            device_id=dev,
            device_id_type=MESH,
        )

    barrier = pltpu.get_barrier_semaphore()
    greeted = [z_next, z_prev] + [(d, tpeer(k)) for k in range(1, TS)]
    fx_peers = [(4 * z + lax.rem(q + k, 4), t) for k in range(1, 4)]
    greeted = greeted + fx_peers
    for dev in greeted:
        pl.semaphore_signal(barrier, inc=1, device_id=dev, device_id_type=MESH)

    own_rows = pl.ds(pl.multiple_of(ROWS * c, 32), ROWS)
    feats[own_rows, :] = feat_ref[...]
    hidden = text_ref[...].astype(F32)
    lifted = layer_norm(hidden, ln_ref[...]).astype(BF16)

    pl.semaphore_wait(barrier, len(greeted))
    feat_copy = rcopy(feats.at[own_rows], feats.at[own_rows], S_FEAT, S_FEAT, c_peer)
    feat_copy.start()

    active = jax.nn.gelu(mm(lifted, up_ref[...]), approximate=True).astype(BF16)

    other_rows = pl.ds(pl.multiple_of(ROWS * (1 - c), 32), ROWS)
    feat_copy.wait_send()
    rcopy(feats.at[other_rows], feats.at[other_rows], S_FEAT, S_FEAT, c_peer).wait_recv()

    part_t[...] = mm(feats[...], vis_ref[...]).T
    img_s[...] = part_t[pl.ds(pl.multiple_of(PIECE * c, 8), PIECE), :].astype(BF16)
    for k in range(1, TS):
        rcopy(img_s, img_r.at[c, t], S_IMG + k, S_IMG + t, (d, tpeer(k))).start()
    img_r[c, t] = img_s[...]

    mixed = mm(active, down_ref[...])
    with_hidden = mixed + hidden
    for j in range(TS):
        mix_s[j] = mixed[TEXTS * j : TEXTS * (j + 1)].astype(BF16)
        mix_f[j] = with_hidden[TEXTS * j : TEXTS * (j + 1)]

    def exchange_start(src, dst, sem):
        for k in range(1, TS):
            rcopy(src.at[tpeer(k)], dst.at[t], sem + k, sem + t, (d, tpeer(k))).start()

    def exchange_wait(src, dst, sem):
        for k in range(1, TS):
            j = tpeer(k)
            rcopy(src.at[j], dst.at[t], sem + k, sem + t, (d, j)).wait_send()
            rcopy(src.at[j], dst.at[j], sem + k, sem + j, (d, j)).wait_recv()

    exchange_start(mix_s, mix_r, S_MIX)
    mix_r[t] = jnp.zeros((TEXTS, D), BF16)

    for k in range(1, TS):
        j = tpeer(k)
        rcopy(img_s, img_r.at[c, t], S_IMG + k, S_IMG + t, (d, j)).wait_send()
        rcopy(img_s, img_r.at[c, j], S_IMG + k, S_IMG + j, (d, j)).wait_recv()
    imgc_copy = rcopy(img_r.at[c], img_r.at[c], S_IMGC, S_IMGC, c_peer)
    imgc_copy.start()

    exchange_wait(mix_s, mix_r, S_MIX)
    total = mix_f[t]
    for j in range(TS):
        total = total + mix_r[j].astype(F32)
    normed = layer_norm(total, fg_ref[...]).astype(BF16).astype(F32)
    for j in range(TS):
        nrm_s[j] = normed[:, COLS * j : COLS * (j + 1)].astype(BF16)
    exchange_start(nrm_s, nrm_r, S_NRM)
    nrm_r[t] = nrm_s[t]
    exchange_wait(nrm_s, nrm_r, S_NRM)
    for j in range(TS):
        nrm_a[TEXTS * j : TEXTS * (j + 1), :] = nrm_r[j].astype(F32)
    head_part = mm(nrm_a[...].astype(BF16), head_ref[...])
    for j in range(TS):
        head_f[j] = head_part[TEXTS * j : TEXTS * (j + 1)]
        head_s[j] = head_part[TEXTS * j : TEXTS * (j + 1)].astype(BF16)
    exchange_start(head_s, head_r, S_HEAD)
    head_r[t] = jnp.zeros((TEXTS, E), BF16)

    imgc_copy.wait_send()
    rcopy(img_r.at[1 - c], img_r.at[1 - c], S_IMGC, S_IMGC, c_peer).wait_recv()
    for j in range(TS):
        for h in range(2):
            at = COLS * j + PIECE * h
            img_f[at : at + PIECE, :] = img_r[h, j].astype(F32)
    emb_t = img_f[...]
    inverse = lax.rsqrt(jnp.sum(emb_t * emb_t, axis=0, keepdims=True) + norm_eps)
    inv_ref[...] = inverse
    unit_t = emb_t * inverse
    img_f[...] = unit_t
    img_ut[...] = unit_t.astype(BF16)
    img_u[...] = unit_t.T.astype(BF16)
    eg[...] = jnp.zeros_like(eg)

    exchange_wait(head_s, head_r, S_HEAD)
    text_emb = head_f[t]
    for j in range(TS):
        text_emb = text_emb + head_r[j].astype(F32)
    text_unit = text_emb * lax.rsqrt(
        jnp.sum(text_emb * text_emb, axis=1, keepdims=True) + norm_eps
    )
    text_unit = text_unit.astype(BF16)
    yh_s[...] = text_unit
    yh_copy = rcopy(yh_s, yh_r, S_YH, S_YH, yh_peer)
    yh_copy.start()
    chunk_f[0:TEXTS, :] = text_unit.astype(F32)
    yh_copy.wait()
    chunk_f[TEXTS:CHUNK, :] = yh_r[...].astype(F32)
    texts[z] = chunk_f[...].astype(BF16)

    def ag_plus(s):
        at = zmod(z - s + 1)
        return rcopy(texts.at[at], texts.at[at], S_AGP + s - 1, S_AGP + s - 1, z_next)

    def ag_minus(s):
        at = zmod(z + s - 1)
        return rcopy(texts.at[at], texts.at[at], S_AGM + s - 1, S_AGM + s - 1, z_prev)

    def ag_plus_in(s):
        at = zmod(z - s)
        return rcopy(texts.at[at], texts.at[at], S_AGP + s - 1, S_AGP + s - 1, z_next)

    def ag_minus_in(s):
        at = zmod(z + s)
        return rcopy(texts.at[at], texts.at[at], S_AGM + s - 1, S_AGM + s - 1, z_prev)

    row_ids = lax.broadcasted_iota(jnp.int32, (CHUNK, IMGS), 0)
    col_ids = lax.broadcasted_iota(jnp.int32, (CHUNK, IMGS), 1)
    diagonal = ((row_ids < TEXTS) & (col_ids == row_ids + ROWS * c + TEXTS * t)).astype(F32)

    def process(origin, own):
        block = texts[origin]
        logits = logit_scale * mm(block, img_ut[...]) + logit_bias
        weights = jax.nn.sigmoid(logits)
        if own:
            weights = weights - diagonal
        weights = (weights * (logit_scale / ROWS)).astype(BF16)
        grads[origin] = mm(weights, img_u[...])
        eg[...] += lax.dot_general(
            block, weights, (((0,), (0,)), ((), ())), preferred_element_type=F32
        )

    ag_plus(1).start()
    ag_minus(1).start()
    process(z, True)

    def ag_step(s, _):
        ag_plus_in(s).wait_recv()
        ag_plus(s + 1).start()
        process(zmod(z - s), False)
        ag_minus_in(s).wait_recv()

        @pl.when(s < HALF - 1)
        def _():
            ag_minus(s + 1).start()

        process(zmod(z + s), False)
        return 0

    lax.fori_loop(1, HALF, ag_step, 0)

    def rs_copy(way, s):
        sem = (S_RSP, S_RSM)[way] + s - 1
        return rcopy(rs_s.at[way, s - 1], rs_r.at[way, s - 1], sem, sem, (z_next, z_prev)[way])

    def rs_step(way, s):
        owner = zmod(z + HALF + 1 - s) if way == 0 else zmod(z - HALF + s)
        value = grads[owner]
        if s > 1:
            rs_copy(way, s - 1).wait_recv()
            value = value + rs_r[way, s - 2].astype(F32)
        rs_s[way, s - 1] = value.astype(BF16)
        rs_copy(way, s).start()

    rs_step(1, 1)
    ag_plus_in(HALF).wait_recv()
    process(zmod(z - HALF), False)
    rs_step(0, 1)

    image_grad = eg[...]
    unit_t = img_f[...]
    radial = jnp.sum(unit_t * image_grad, axis=0, keepdims=True)
    eg[...] = (image_grad - unit_t * radial) * inv_ref[...]
    for j in range(TS):
        theirs = pl.ds(pl.multiple_of(COLS * j + PIECE * (1 - c), 8), PIECE)
        cx_s[j] = eg[theirs, :].astype(BF16)
    cx_copy = rcopy(cx_s, cx_r, S_CX, S_CX, c_peer)
    cx_copy.start()
    rs_step(1, 2)
    rs_step(0, 2)
    cx_copy.wait()
    for j in range(TS):
        mine = pl.ds(pl.multiple_of(COLS * j + PIECE * c, 8), PIECE)
        value = eg[mine, :] + cx_r[j].astype(F32)
        px_f[j] = value
        px_s[j] = value.astype(BF16)
    exchange_start(px_s, px_r, S_PX)
    px_r[t] = jnp.zeros((PIECE, IMGS), BF16)
    rs_step(1, 3)
    rs_step(0, 3)
    rs_step(1, 4)
    rs_step(0, 4)
    exchange_wait(px_s, px_r, S_PX)
    emb_grad = px_f[t]
    for j in range(TS):
        emb_grad = emb_grad + px_r[j].astype(F32)
    vg_all[...] = mm(emb_grad.astype(BF16), feats[...]).T

    def vr_copy(way, s):
        sem = (S_VRP, S_VRM)[way] + s - 1
        return rcopy(vr_s.at[way, s - 1], vr_r.at[way, s - 1], sem, sem, (z_next, z_prev)[way])

    def vg_chunk(owner):
        return vg_all[pl.ds(pl.multiple_of(ZROWS * owner, 8), ZROWS), :]

    def vr_step(way, s):
        owner = zmod(z + HALF + 1 - s) if way == 0 else zmod(z - HALF + s)
        value = vg_chunk(owner)
        if s > 1:
            vr_copy(way, s - 1).wait_recv()
            value = value + vr_r[way, s - 2]
        vr_s[way, s - 1] = value
        vr_copy(way, s).start()

    for s in range(1, HALF + 1):
        vr_step(0, s)
        if s < HALF:
            vr_step(1, s)
        r = s + 4
        if r <= HALF:
            if r < HALF:
                rs_step(1, r)
            rs_step(0, r)
        if r == HALF + 1:
            rs_copy(0, HALF).wait_recv()
            rs_copy(1, HALF - 1).wait_recv()
            chunk_f[...] = (
                grads[z] + rs_r[0, HALF - 1].astype(F32) + rs_r[1, HALF - 2].astype(F32)
            )
            yg_s[...] = chunk_f[TEXTS:CHUNK, :]
            rcopy(yg_s, yg_r, S_YG, S_YG, yh_peer).start()

    rcopy(yg_s, yg_r, S_YG, S_YG, yh_peer).wait()
    tg_ref[...] = chunk_f[0:TEXTS, :] + yg_r[...]

    vr_copy(0, HALF).wait_recv()
    vr_copy(1, HALF - 1).wait_recv()
    fx[q] = vg_chunk(z) + vr_r[0, HALF - 1] + vr_r[1, HALF - 2]
    for k in range(1, 4):
        rcopy(fx.at[q], fx.at[q], S_FX + k, S_FX + q, fx_peers[k - 1]).start()

    def ag_drain(s, _):
        ag_plus(s).wait_send()

        @pl.when(s < HALF)
        def _():
            ag_minus(s).wait_send()

        return 0

    lax.fori_loop(1, HALF + 1, ag_drain, 0)
    for s in range(1, HALF + 1):
        for way in range(2):
            if s < HALF or way == 0:
                rs_copy(way, s).wait_send()
                vr_copy(way, s).wait_send()

    for k in range(1, 4):
        o = lax.rem(q + k, 4)
        rcopy(fx.at[q], fx.at[q], S_FX + k, S_FX + q, fx_peers[k - 1]).wait_send()
        rcopy(fx.at[o], fx.at[o], S_FX + k, S_FX + o, fx_peers[k - 1]).wait_recv()
    left = fx[0] + fx[2]
    right = fx[1] + fx[3]
    for k in range(4):

        @pl.when(q == k)
        def _():
            vg_ref[:, 0:PIECE] = left[18 * k : 18 * (k + 1), :]
            vg_ref[:, PIECE:COLS] = right[18 * k : 18 * (k + 1), :]


def local(
    text_hidden,
    ln_gain,
    up_weight,
    down_weight,
    final_gain,
    head_weight,
    image_features,
    vision_weight,
):
    vmem = pl.BlockSpec(memory_space=pltpu.VMEM)
    scratch = [
        ((IMGS, D), BF16),
        ((COLS, IMGS), F32),
        ((PIECE, IMGS), BF16),
        ((2, TS, PIECE, IMGS), BF16),
        ((E, IMGS), F32),
        ((E, IMGS), BF16),
        ((IMGS, E), BF16),
        ((1, IMGS), F32),
        ((TS, TEXTS, D), BF16),
        ((TS, TEXTS, D), F32),
        ((TS, TEXTS, D), BF16),
        ((TS, TEXTS, COLS), BF16),
        ((TS, TEXTS, COLS), BF16),
        ((ROWS, COLS), F32),
        ((TS, TEXTS, E), BF16),
        ((TS, TEXTS, E), F32),
        ((TS, TEXTS, E), BF16),
        ((TEXTS, E), BF16),
        ((TEXTS, E), BF16),
        ((CHUNK, E), F32),
        ((ZS, CHUNK, E), BF16),
        ((ZS, CHUNK, E), F32),
        ((E, IMGS), F32),
        ((2, HALF, CHUNK, E), BF16),
        ((2, HALF, CHUNK, E), BF16),
        ((TEXTS, E), F32),
        ((TEXTS, E), F32),
        ((TS, PIECE, IMGS), BF16),
        ((TS, PIECE, IMGS), BF16),
        ((TS, PIECE, IMGS), F32),
        ((TS, PIECE, IMGS), BF16),
        ((TS, PIECE, IMGS), BF16),
        ((D, PIECE), F32),
        ((2, HALF, ZROWS, PIECE), F32),
        ((2, HALF, ZROWS, PIECE), F32),
        ((4, ZROWS, PIECE), F32),
    ]
    return pl.pallas_call(
        kernel,
        out_shape=(
            jax.ShapeDtypeStruct((TEXTS, E), F32),
            jax.ShapeDtypeStruct((D // 64, COLS), F32),
        ),
        in_specs=[vmem] * 8,
        out_specs=(vmem, vmem),
        scratch_shapes=[pltpu.VMEM(shape, kind) for shape, kind in scratch]
        + [pltpu.SemaphoreType.DMA((S_ALL,)), pltpu.SemaphoreType.DMA((S_ALL,))],
        compiler_params=pltpu.CompilerParams(
            collective_id=0, has_side_effects=True, vmem_limit_bytes=56 * 1024 * 1024
        ),
    )(
        text_hidden,
        ln_gain.reshape(1, D),
        up_weight,
        down_weight,
        final_gain.reshape(1, D),
        head_weight,
        image_features,
        vision_weight,
    )


def solution(mesh):
    placed = (
        P("dp", None),
        P(),
        P(None, "tensor"),
        P("tensor", None),
        P(),
        P("tensor", None),
        P("dp", None),
        P(None, "tensor"),
    )
    return jax.shard_map(
        local,
        mesh=mesh,
        in_specs=placed,
        out_specs=(P(("dp", "tensor"), None), P("dp", "tensor")),
        check_vma=False,
    )
```

time: 1660 us -> 140 us (0.08)
  waiting for transfers between devices: 959 us -> 0 us
  starting transfers between devices: 278 us -> 0 us
  local copies, waits for them, and re-layouts: 194 us -> 10.1 us
  Pallas kernels: 0 us -> 129 us
  matrix products: 110 us -> 0 us
  other arithmetic: 56.4 us -> 0 us
  blocking collectives: 32.9 us -> 0 us
    unnamed x5 -> x0, waiting for transfers between devices: 482 us -> none
    ppermute x127 -> x0, starting transfers between devices: 278 us -> none  [from_behind(): return lax.ppermute(block, axis, route)]
    ppermute x127 -> x0, waiting for transfers between devices: 277 us -> none  [from_behind(): return lax.ppermute(block, axis, route)]
    dynamic_update_slice x128 -> x0, local copies, waits for them, and re-layouts: 188 us -> none  [the longest x63 98.2 us: visit_block(): blocks = lax.dynamic_update_slice_in_dim(blocks, text_block, offset, 0)]
    psum x2 -> x0, waiting for transfers between devices: 153 us -> none  [the longest x1 90.4 us: local(): head_total = lax.psum(head_part, 'tensor')]
    pallas_call x0 -> x1, Pallas kernels: none -> 129 us  [local(): pl.pallas_call(kernel, out_shape=(jax.ShapeDtypeStruct((TEXTS, E), F32),...]
    dot_general x133 -> x0, matrix products: 110 us -> none  [the longest x129 102 us: contract(): lax.dot_general(left_side, right_side, (((left_dim,), (right_dim,)), ((),...]
    add x32 -> x0, other arithmetic: 48.1 us -> none  [the longest x31 48.1 us: visit_block(): return (text_block, grad_block + text_term, coefs, blocks)]
  transfers between devices with their start and end apart: 131 -> 0, of which waited for: 93 -> 0; matrix products, arithmetic and copies ran while one was open for 17% -> 0% of each run, Pallas kernels for 0% -> 0%
where the time goes in v1:
time: 140 us
  Pallas kernels  129 us (92%)
  local copies, waits for them, and re-layouts  10.1 us (7%)
    pallas_call x1, Pallas kernels, local(): pl.pallas_call(kernel, out_shape=(jax.ShapeDtypeStruct((TEXTS, E), F32),...  129 us
    unnamed x4, local copies, waits for them, and re-layouts  7.56 us

profile of v1, /device:TPU:1, one launch (start us, length us, event | category | flops | bytes accessed | tf_op | source)
XLA Modules:
  0.0 139.6 jit_solution(361107375452583937)
XLA Ops:
  0.6 1.3 reshape.10.ln_ref
  1.9 1.3 reshape.11.fg_ref
  3.2 2.1 %copy.11.vis_ref = bf16[1152,144]{1,0:T(8,128)(2,1)} copy(bf16[1152,144]{0,1:T(8,128)(2,1)} %param.15) | data formatting | bytes 663552 | tf_op args[7]
  5.3 2.6 %copy.10.up_ref = bf16[1152,538]{1,0:T(8,128)(2,1)} copy(bf16[1152,538]{0,1:T(8,128)(2,1)} %param.10) | data formatting | bytes 2479104 | tf_op args[2]
  7.9 128.8 %shard_map.95 = (f32[20,1152]{1,0:T(8,128)}, f32[18,144]{1,0:T(8,128)}) custom-call(bf16[160,1152]{1,0:T(8,128)(2,1)} %text_ref.1, f32[1,1152]{1,0:T(1,128)} %reshape.10.ln_ref, bf16[1152,538]{1,0:T(8,128)(2,1)} %copy.10.up_ref, bf16[538,1152]{1,0:T(8,128)(2,1)} %down_ref.1, f32[1,1152]{1,0:T(1,128)} %reshape.11.fg_ref, bf16[144,1152]{1,0:T(8,128)(2,1)} %head_ref.1, ...), custom_call_target="tpu_custom_call" | custom-call | tf_op jit(solution)/shard_map/pallas_call | solution.py:463
  136.7 1.5 %copy.14 = f32[20,1152]{1,0:T(8,128)} copy(f32[20,1152]{1,0:T(8,128)} %get-tuple-element.4) | data formatting | bytes 184320
  138.3 1.3 copy.15

commit v2 on v1

--- a/solution.py
+++ b/solution.py
@@ -20,6 +20,7 @@
 TS = 8
 ZS = 16
 HALF = ZS // 2
+FF_DEV = 4304 // TS
 TEXTS = ROWS // TS
 CHUNK = 2 * TEXTS
 IMGS = 2 * ROWS
@@ -30,6 +31,10 @@
 
 def mm(a, b):
     return jnp.dot(a, b, preferred_element_type=F32)
+
+
+def mm_t(a, b):
+    return lax.dot_general(a, b, (((1,), (1,)), ((), ())), preferred_element_type=F32)
 
 
 def layer_norm(values, gain_row):
@@ -45,17 +50,16 @@
 S_NRM = S_MIX + TS
 S_HEAD = S_NRM + TS
 S_YH = S_HEAD + TS
-S_AGP = S_YH + 1
-S_AGM = S_AGP + HALF
-S_RSP = S_AGM + HALF
-S_RSM = S_RSP + HALF
-S_YG = S_RSM + HALF
+S_AG = S_YH + 1
+S_RS = S_AG + 4 * HALF
+S_YG = S_RS + 4 * HALF
 S_CX = S_YG + 1
 S_PX = S_CX + 1
 S_VRP = S_PX + TS
 S_VRM = S_VRP + HALF
 S_FX = S_VRM + HALF
 S_ALL = S_FX + 4
+L_FEAT, L_UP, L_DOWN, L_HEAD, L_VIS = range(5)
 
 
 def kernel(
@@ -69,6 +73,10 @@
     vis_ref,
     tg_ref,
     vg_ref,
+    up_v,
+    down_v,
+    head_v,
+    vis_v,
     feats,
     part_t,
     img_s,
@@ -86,9 +94,7 @@
     head_s,
     head_f,
     head_r,
-    yh_s,
-    yh_r,
-    chunk_f,
+    block_f,
     texts,
     grads,
     eg,
@@ -107,6 +113,7 @@
     fx,
     send_sem,
     recv_sem,
+    load_sem,
 ):
     d = lax.axis_index("dp")
     t = lax.axis_index("tensor")
@@ -144,31 +151,32 @@
         pl.semaphore_signal(barrier, inc=1, device_id=dev, device_id_type=MESH)
 
     own_rows = pl.ds(pl.multiple_of(ROWS * c, 32), ROWS)
-    feats[own_rows, :] = feat_ref[...]
+    other_rows = pl.ds(pl.multiple_of(ROWS * (1 - c), 32), ROWS)
+    loads = [
+        pltpu.make_async_copy(src, dst, load_sem.at[at])
+        for at, (src, dst) in enumerate(
+            [
+                (feat_ref, feats.at[own_rows]),
+                (up_ref, up_v),
+                (down_ref, down_v),
+                (head_ref, head_v),
+                (vis_ref, vis_v),
+            ]
+        )
+    ]
+    for at in (L_UP, L_DOWN, L_FEAT, L_VIS, L_HEAD):
+        loads[at].start()
+
     hidden = text_ref[...].astype(F32)
-    lifted = layer_norm(hidden, ln_ref[...]).astype(BF16)
+    lifted = layer_norm(hidden, ln_ref[...].reshape(1, D)).astype(BF16)
+    loads[L_UP].wait()
+    active = jax.nn.gelu(mm_t(lifted, up_v[...]), approximate=True).astype(BF16)
+    loads[L_DOWN].wait()
+    mixed = mm(active, down_v[...])
+    for j in range(TS):
+        mix_s[j] = mixed[TEXTS * j : TEXTS * (j + 1)].astype(BF16)
 
     pl.semaphore_wait(barrier, len(greeted))
-    feat_copy = rcopy(feats.at[own_rows], feats.at[own_rows], S_FEAT, S_FEAT, c_peer)
-    feat_copy.start()
-
-    active = jax.nn.gelu(mm(lifted, up_ref[...]), approximate=True).astype(BF16)
-
-    other_rows = pl.ds(pl.multiple_of(ROWS * (1 - c), 32), ROWS)
-    feat_copy.wait_send()
-    rcopy(feats.at[other_rows], feats.at[other_rows], S_FEAT, S_FEAT, c_peer).wait_recv()
-
-    part_t[...] = mm(feats[...], vis_ref[...]).T
-    img_s[...] = part_t[pl.ds(pl.multiple_of(PIECE * c, 8), PIECE), :].astype(BF16)
-    for k in range(1, TS):
-        rcopy(img_s, img_r.at[c, t], S_IMG + k, S_IMG + t, (d, tpeer(k))).start()
-    img_r[c, t] = img_s[...]
-
-    mixed = mm(active, down_ref[...])
-    with_hidden = mixed + hidden
-    for j in range(TS):
-        mix_s[j] = mixed[TEXTS * j : TEXTS * (j + 1)].astype(BF16)
-        mix_f[j] = with_hidden[TEXTS * j : TEXTS * (j + 1)]
 
     def exchange_start(src, dst, sem):
         for k in range(1, TS):
@@ -181,7 +189,32 @@
             rcopy(src.at[j], dst.at[j], sem + k, sem + j, (d, j)).wait_recv()
 
     exchange_start(mix_s, mix_r, S_MIX)
+    loads[L_FEAT].wait()
+    feat_copy = rcopy(feats.at[own_rows], feats.at[own_rows], S_FEAT, S_FEAT, c_peer)
+    feat_copy.start()
     mix_r[t] = jnp.zeros((TEXTS, D), BF16)
+    with_hidden = mixed + hidden
+    for j in range(TS):
+        mix_f[j] = with_hidden[TEXTS * j : TEXTS * (j + 1)]
+
+    loads[L_VIS].wait()
+    feat_copy.wait_send()
+    rcopy(feats.at[other_rows], feats.at[other_rows], S_FEAT, S_FEAT, c_peer).wait_recv()
+    part_t[...] = mm_t(vis_v[...], feats[...])
+    img_s[...] = part_t[pl.ds(pl.multiple_of(PIECE * c, 8), PIECE), :].astype(BF16)
+    for k in range(1, TS):
+        rcopy(img_s, img_r.at[c, t], S_IMG + k, S_IMG + t, (d, tpeer(k))).start()
+    img_r[c, t] = img_s[...]
+
+    exchange_wait(mix_s, mix_r, S_MIX)
+    total = mix_f[t]
+    for j in range(TS):
+        total = total + mix_r[j].astype(F32)
+    normed = layer_norm(total, fg_ref[...].reshape(1, D)).astype(BF16).astype(F32)
+    for j in range(TS):
+        nrm_s[j] = normed[:, COLS * j : COLS * (j + 1)].astype(BF16)
+    exchange_start(nrm_s, nrm_r, S_NRM)
+    nrm_r[t] = nrm_s[t]
 
     for k in range(1, TS):
         j = tpeer(k)
@@ -190,19 +223,11 @@
     imgc_copy = rcopy(img_r.at[c], img_r.at[c], S_IMGC, S_IMGC, c_peer)
     imgc_copy.start()
 
-    exchange_wait(mix_s, mix_r, S_MIX)
-    total = mix_f[t]
-    for j in range(TS):
-        total = total + mix_r[j].astype(F32)
-    normed = layer_norm(total, fg_ref[...]).astype(BF16).astype(F32)
-    for j in range(TS):
-        nrm_s[j] = normed[:, COLS * j : COLS * (j + 1)].astype(BF16)
-    exchange_start(nrm_s, nrm_r, S_NRM)
-    nrm_r[t] = nrm_s[t]
     exchange_wait(nrm_s, nrm_r, S_NRM)
     for j in range(TS):
         nrm_a[TEXTS * j : TEXTS * (j + 1), :] = nrm_r[j].astype(F32)
-    head_part = mm(nrm_a[...].astype(BF16), head_ref[...])
+    loads[L_HEAD].wait()
+    head_part = mm(nrm_a[...].astype(BF16), head_v[...])
     for j in range(TS):
         head_f[j] = head_part[TEXTS * j : TEXTS * (j + 1)]
         head_s[j] = head_part[TEXTS * j : TEXTS * (j + 1)].astype(BF16)
@@ -231,83 +256,90 @@
     text_unit = text_emb * lax.rsqrt(
         jnp.sum(text_emb * text_emb, axis=1, keepdims=True) + norm_eps
     )
-    text_unit = text_unit.astype(BF16)
-    yh_s[...] = text_unit
-    yh_copy = rcopy(yh_s, yh_r, S_YH, S_YH, yh_peer)
+    texts[0, 0, 0] = text_unit.astype(BF16)
+
+    def ag_copy(s, way, half):
+        source = texts.at[0, 0, half] if isinstance(s, int) and s == 1 else texts.at[s - 1, way, half]
+        sem = S_AG + 4 * (s - 1) + 2 * way + half
+        return rcopy(source, texts.at[s, way, half], sem, sem, (z_next, z_prev)[way])
+
+    yh_copy = rcopy(texts.at[0, 0, 0], texts.at[0, 0, 1], S_YH, S_YH, yh_peer)
+    ag_copy(1, 0, 0).start()
+    ag_copy(1, 1, 0).start()
     yh_copy.start()
-    chunk_f[0:TEXTS, :] = text_unit.astype(F32)
-    yh_copy.wait()
-    chunk_f[TEXTS:CHUNK, :] = yh_r[...].astype(F32)
-    texts[z] = chunk_f[...].astype(BF16)
-
-    def ag_plus(s):
-        at = zmod(z - s + 1)
-        return rcopy(texts.at[at], texts.at[at], S_AGP + s - 1, S_AGP + s - 1, z_next)
-
-    def ag_minus(s):
-        at = zmod(z + s - 1)
-        return rcopy(texts.at[at], texts.at[at], S_AGM + s - 1, S_AGM + s - 1, z_prev)
-
-    def ag_plus_in(s):
-        at = zmod(z - s)
-        return rcopy(texts.at[at], texts.at[at], S_AGP + s - 1, S_AGP + s - 1, z_next)
-
-    def ag_minus_in(s):
-        at = zmod(z + s)
-        return rcopy(texts.at[at], texts.at[at], S_AGM + s - 1, S_AGM + s - 1, z_prev)
 
     row_ids = lax.broadcasted_iota(jnp.int32, (CHUNK, IMGS), 0)
     col_ids = lax.broadcasted_iota(jnp.int32, (CHUNK, IMGS), 1)
     diagonal = ((row_ids < TEXTS) & (col_ids == row_ids + ROWS * c + TEXTS * t)).astype(F32)
 
-    def process(origin, own):
-        block = texts[origin]
+    def process(s, pieces):
+        rows = TEXTS * len(pieces)
+        for at, (way, half) in enumerate(pieces):
+            block_f[TEXTS * at : TEXTS * (at + 1), :] = texts[s, way, half].astype(F32)
+        block = block_f[0:rows, :].astype(BF16)
         logits = logit_scale * mm(block, img_ut[...]) + logit_bias
         weights = jax.nn.sigmoid(logits)
-        if own:
+        if isinstance(s, int) and s == 0:
             weights = weights - diagonal
         weights = (weights * (logit_scale / ROWS)).astype(BF16)
-        grads[origin] = mm(weights, img_u[...])
         eg[...] += lax.dot_general(
             block, weights, (((0,), (0,)), ((), ())), preferred_element_type=F32
         )
-
-    ag_plus(1).start()
-    ag_minus(1).start()
-    process(z, True)
+        grads[s, 0:rows, :] = mm(weights, img_u[...])
+
+    yh_copy.wait()
+    ag_copy(1, 0, 1).start()
+    ag_copy(1, 1, 1).start()
+    process(0, ((0, 0), (0, 1)))
 
     def ag_step(s, _):
-        ag_plus_in(s).wait_recv()
-        ag_plus(s + 1).start()
-        process(zmod(z - s), False)
-        ag_minus_in(s).wait_recv()
-
-        @pl.when(s < HALF - 1)
-        def _():
-            ag_minus(s + 1).start()
-
-        process(zmod(z + s), False)
+        for half in range(2):
+            for way in range(2):
+                ag_copy(s, way, half).wait_recv()
+                if half == way:
+                    ag_copy(s + 1, way, half).start()
+                else:
+
+                    @pl.when(s < HALF - 1)
+                    def _():
+                        ag_copy(s + 1, way, half).start()
+
+        process(s, ((0, 0), (0, 1), (1, 0), (1, 1)))
         return 0
 
     lax.fori_loop(1, HALF, ag_step, 0)
 
-    def rs_copy(way, s):
-        sem = (S_RSP, S_RSM)[way] + s - 1
-        return rcopy(rs_s.at[way, s - 1], rs_r.at[way, s - 1], sem, sem, (z_next, z_prev)[way])
+    def rs_copy(way, s, half):
+        sem = S_RS + 4 * (s - 1) + 2 * way + half
+        return rcopy(
+            rs_s.at[way, s - 1, half], rs_r.at[way, s - 1, half], sem, sem, (z_next, z_prev)[way]
+        )
+
+    def rs_halves(way, s):
+        return (way,) if s == 1 else (1, 0)
 
     def rs_step(way, s):
-        owner = zmod(z + HALF + 1 - s) if way == 0 else zmod(z - HALF + s)
-        value = grads[owner]
-        if s > 1:
-            rs_copy(way, s - 1).wait_recv()
-            value = value + rs_r[way, s - 2].astype(F32)
-        rs_s[way, s - 1] = value.astype(BF16)
-        rs_copy(way, s).start()
-
+        for half in rs_halves(way, s):
+            first = TEXTS * half if s == 1 else CHUNK * (1 - way) + TEXTS * half
+            value = grads[HALF + 1 - s, first : first + TEXTS, :]
+            if s > 1 and half in rs_halves(way, s - 1):
+                rs_copy(way, s - 1, half).wait_recv()
+                value = value + rs_r[way, s - 2, half].astype(F32)
+            rs_s[way, s - 1, half] = value.astype(BF16)
+            rs_copy(way, s, half).start()
+
+    def rs_last(half):
+        value = grads[0, TEXTS * half : TEXTS * (half + 1), :]
+        for way in range(2):
+            rs_copy(way, HALF, half).wait_recv()
+            value = value + rs_r[way, HALF - 1, half].astype(F32)
+        return value
+
+    ag_copy(HALF, 0, 0).wait_recv()
+    ag_copy(HALF, 1, 1).wait_recv()
+    process(HALF, ((0, 0), (1, 1)))
+    rs_step(0, 1)
     rs_step(1, 1)
-    ag_plus_in(HALF).wait_recv()
-    process(zmod(z - HALF), False)
-    rs_step(0, 1)
 
     image_grad = eg[...]
     unit_t = img_f[...]
@@ -360,20 +392,15 @@
             vr_step(1, s)
         r = s + 4
         if r <= HALF:
-            if r < HALF:
-                rs_step(1, r)
+            rs_step(1, r)
             rs_step(0, r)
         if r == HALF + 1:
-            rs_copy(0, HALF).wait_recv()
-            rs_copy(1, HALF - 1).wait_recv()
-            chunk_f[...] = (
-                grads[z] + rs_r[0, HALF - 1].astype(F32) + rs_r[1, HALF - 2].astype(F32)
-            )
-            yg_s[...] = chunk_f[TEXTS:CHUNK, :]
+            yg_s[...] = rs_last(1)
             rcopy(yg_s, yg_r, S_YG, S_YG, yh_peer).start()
 
+    own_grad = rs_last(0)
     rcopy(yg_s, yg_r, S_YG, S_YG, yh_peer).wait()
-    tg_ref[...] = chunk_f[0:TEXTS, :] + yg_r[...]
+    tg_ref[...] = own_grad + yg_r[...]
 
     vr_copy(0, HALF).wait_recv()
     vr_copy(1, HALF - 1).wait_recv()
@@ -381,20 +408,29 @@
     for k in range(1, 4):
         rcopy(fx.at[q], fx.at[q], S_FX + k, S_FX + q, fx_peers[k - 1]).start()
 
+    for half in range(2):
+        for way in range(2):
+            ag_copy(1, way, half).wait_send()
+
     def ag_drain(s, _):
-        ag_plus(s).wait_send()
-
-        @pl.when(s < HALF)
-        def _():
-            ag_minus(s).wait_send()
+        for half in range(2):
+            for way in range(2):
+                if half == way:
+                    ag_copy(s, way, half).wait_send()
+                else:
+
+                    @pl.when(s < HALF)
+                    def _():
+                        ag_copy(s, way, half).wait_send()
 
         return 0
 
-    lax.fori_loop(1, HALF + 1, ag_drain, 0)
+    lax.fori_loop(2, HALF + 1, ag_drain, 0)
     for s in range(1, HALF + 1):
         for way in range(2):
+            for half in rs_halves(way, s):
+                rs_copy(way, s, half).wait_send()
             if s < HALF or way == 0:
-                rs_copy(way, s).wait_send()
                 vr_copy(way, s).wait_send()
 
     for k in range(1, 4):
@@ -422,7 +458,12 @@
     vision_weight,
 ):
     vmem = pl.BlockSpec(memory_space=pltpu.VMEM)
+    hbm = pl.BlockSpec(memory_space=pl.ANY)
     scratch = [
+        ((FF_DEV, D), BF16),
+        ((FF_DEV, D), BF16),
+        ((COLS, E), BF16),
+        ((COLS, D), BF16),
         ((IMGS, D), BF16),
         ((COLS, IMGS), F32),
         ((PIECE, IMGS), BF16),
@@ -440,14 +481,12 @@
         ((TS, TEXTS, E), BF16),
         ((TS, TEXTS, E), F32),
         ((TS, TEXTS, E), BF16),
-        ((TEXTS, E), BF16),
-        ((TEXTS, E), BF16),
-        ((CHUNK, E), F32),
-        ((ZS, CHUNK, E), BF16),
-        ((ZS, CHUNK, E), F32),
+        ((2 * CHUNK, E), F32),
+        ((HALF + 1, 2, 2, TEXTS, E), BF16),
+        ((HALF + 1, 2 * CHUNK, E), F32),
         ((E, IMGS), F32),
-        ((2, HALF, CHUNK, E), BF16),
-        ((2, HALF, CHUNK, E), BF16),
+        ((2, HALF, 2, TEXTS, E), BF16),
+        ((2, HALF, 2, TEXTS, E), BF16),
         ((TEXTS, E), F32),
         ((TEXTS, E), F32),
         ((TS, PIECE, IMGS), BF16),
@@ -466,22 +505,22 @@
             jax.ShapeDtypeStruct((TEXTS, E), F32),
             jax.ShapeDtypeStruct((D // 64, COLS), F32),
         ),
-        in_specs=[vmem] * 8,
+        in_specs=[vmem, vmem, hbm, hbm, vmem, hbm, hbm, hbm],
         out_specs=(vmem, vmem),
         scratch_shapes=[pltpu.VMEM(shape, kind) for shape, kind in scratch]
-        + [pltpu.SemaphoreType.DMA((S_ALL,)), pltpu.SemaphoreType.DMA((S_ALL,))],
+        + [pltpu.SemaphoreType.DMA((size,)) for size in (S_ALL, S_ALL, 5)],
         compiler_params=pltpu.CompilerParams(
             collective_id=0, has_side_effects=True, vmem_limit_bytes=56 * 1024 * 1024
         ),
     )(
         text_hidden,
-        ln_gain.reshape(1, D),
-        up_weight,
+        ln_gain,
+        up_weight.T,
         down_weight,
-        final_gain.reshape(1, D),
+        final_gain,
         head_weight,
         image_features,
-        vision_weight,
+        vision_weight.T,
     )
 
 

time: 140 us -> 121 us (0.86)
  Pallas kernels: 129 us -> 117 us
  local copies, waits for them, and re-layouts: 10.1 us -> 2.9 us
    pallas_call x1, Pallas kernels: 129 us -> 117 us  [local(): pl.pallas_call(kernel, out_shape=(jax.ShapeDtypeStruct((TEXTS, E), F32),...]
    unnamed x4 -> x2, local copies, waits for them, and re-layouts: 7.56 us -> 2.9 us
    reshape x2 -> x0, local copies, waits for them, and re-layouts: 2.59 us -> none  [the longest x1 1.29 us: local(): ln_gain.reshape(1, D)]
where the time goes in v2:
time: 121 us
  Pallas kernels  117 us (97%)
  local copies, waits for them, and re-layouts  2.9 us (2%)
    pallas_call x1, Pallas kernels, local(): pl.pallas_call(kernel, out_shape=(jax.ShapeDtypeStruct((TEXTS, E), F32),...  117 us
    unnamed x2, local copies, waits for them, and re-layouts  2.9 us

profile of v2, /device:TPU:1, one launch (start us, length us, event | category | flops | bytes accessed | tf_op | source)
XLA Modules:
  0.0 120.8 jit_solution(12723465860270514938)
XLA Ops:
  0.6 117.2 %shard_map.95 = (f32[20,1152]{1,0:T(8,128)}, f32[18,144]{1,0:T(8,128)}) custom-call(bf16[160,1152]{1,0:T(8,128)(2,1)} %text_ref.1, f32[1152]{0:T(1024)} %ln_ref.1, bf16[538,1152]{1,0:T(8,128)(2,1)} %bitcast.2, bf16[538,1152]{1,0:T(8,128)(2,1)} %down_ref.1, f32[1152]{0:T(1024)} %fg_ref.1, bf16[144,1152]{1,0:T(8,128)(2,1)} %head_ref.1, ...), custom_call_target="tpu_custom_call" | custom-call | tf_op jit(solution)/shard_map/pallas_call | solution.py:502
  117.9 1.5 %copy.12 = f32[20,1152]{1,0:T(8,128)} copy(f32[20,1152]{1,0:T(8,128)} %get-tuple-element.4) | data formatting | bytes 184320
  119.4 1.3 %copy.13 = f32[18,144]{1,0:T(8,128)} copy(f32[18,144]{1,0:T(8,128)} %get-tuple-element.5) | data formatting | bytes 20736

commit v3 on v2

--- a/solution.py
+++ b/solution.py
@@ -23,9 +23,10 @@
 FF_DEV = 4304 // TS
 TEXTS = ROWS // TS
 CHUNK = 2 * TEXTS
-IMGS = 2 * ROWS
+IMGS = 384
 PIECE = E // (2 * TS)
 COLS = E // TS
+WIDE = 128
 ZROWS = D // ZS
 
 
@@ -54,7 +55,7 @@
 S_RS = S_AG + 4 * HALF
 S_YG = S_RS + 4 * HALF
 S_CX = S_YG + 1
-S_PX = S_CX + 1
+S_PX = S_CX + TS
 S_VRP = S_PX + TS
 S_VRM = S_VRP + HALF
 S_FX = S_VRM + HALF
@@ -85,6 +86,7 @@
     img_ut,
     img_u,
     inv_ref,
+    rad_ref,
     mix_s,
     mix_f,
     mix_r,
@@ -107,6 +109,7 @@
     px_f,
     px_s,
     px_r,
+    emb_b,
     vg_all,
     vr_s,
     vr_r,
@@ -152,6 +155,7 @@
 
     own_rows = pl.ds(pl.multiple_of(ROWS * c, 32), ROWS)
     other_rows = pl.ds(pl.multiple_of(ROWS * (1 - c), 32), ROWS)
+    feats[2 * ROWS : IMGS, :] = jnp.zeros((IMGS - 2 * ROWS, D), BF16)
     loads = [
         pltpu.make_async_copy(src, dst, load_sem.at[at])
         for at, (src, dst) in enumerate(
@@ -216,23 +220,23 @@
     exchange_start(nrm_s, nrm_r, S_NRM)
     nrm_r[t] = nrm_s[t]
 
+    exchange_wait(nrm_s, nrm_r, S_NRM)
+    for j in range(TS):
+        nrm_a[TEXTS * j : TEXTS * (j + 1), :] = nrm_r[j].astype(F32)
+    loads[L_HEAD].wait()
+    head_part = mm(nrm_a[...].astype(BF16), head_v[...])
+    for j in range(TS):
+        head_f[j] = head_part[TEXTS * j : TEXTS * (j + 1)]
+        head_s[j] = head_part[TEXTS * j : TEXTS * (j + 1)].astype(BF16)
+    exchange_start(head_s, head_r, S_HEAD)
+    head_r[t] = jnp.zeros((TEXTS, E), BF16)
+
     for k in range(1, TS):
         j = tpeer(k)
         rcopy(img_s, img_r.at[c, t], S_IMG + k, S_IMG + t, (d, j)).wait_send()
         rcopy(img_s, img_r.at[c, j], S_IMG + k, S_IMG + j, (d, j)).wait_recv()
     imgc_copy = rcopy(img_r.at[c], img_r.at[c], S_IMGC, S_IMGC, c_peer)
     imgc_copy.start()
-
-    exchange_wait(nrm_s, nrm_r, S_NRM)
-    for j in range(TS):
-        nrm_a[TEXTS * j : TEXTS * (j + 1), :] = nrm_r[j].astype(F32)
-    loads[L_HEAD].wait()
-    head_part = mm(nrm_a[...].astype(BF16), head_v[...])
-    for j in range(TS):
-        head_f[j] = head_part[TEXTS * j : TEXTS * (j + 1)]
-        head_s[j] = head_part[TEXTS * j : TEXTS * (j + 1)].astype(BF16)
-    exchange_start(head_s, head_r, S_HEAD)
-    head_r[t] = jnp.zeros((TEXTS, E), BF16)
 
     imgc_copy.wait_send()
     rcopy(img_r.at[1 - c], img_r.at[1 - c], S_IMGC, S_IMGC, c_peer).wait_recv()
@@ -246,8 +250,6 @@
     unit_t = emb_t * inverse
     img_f[...] = unit_t
     img_ut[...] = unit_t.astype(BF16)
-    img_u[...] = unit_t.T.astype(BF16)
-    eg[...] = jnp.zeros_like(eg)
 
     exchange_wait(head_s, head_r, S_HEAD)
     text_emb = head_f[t]
@@ -277,16 +279,24 @@
         for at, (way, half) in enumerate(pieces):
             block_f[TEXTS * at : TEXTS * (at + 1), :] = texts[s, way, half].astype(F32)
         block = block_f[0:rows, :].astype(BF16)
-        logits = logit_scale * mm(block, img_ut[...]) + logit_bias
-        weights = jax.nn.sigmoid(logits)
+        dots = mm(block, img_ut[...])
+        weights = jax.nn.sigmoid(logit_scale * dots + logit_bias)
         if isinstance(s, int) and s == 0:
             weights = weights - diagonal
         weights = (weights * (logit_scale / ROWS)).astype(BF16)
-        eg[...] += lax.dot_general(
+        radial = jnp.sum(weights.astype(F32) * dots, axis=0, keepdims=True)
+        terms = lax.dot_general(
             block, weights, (((0,), (0,)), ((), ())), preferred_element_type=F32
         )
+        if isinstance(s, int) and s == 0:
+            rad_ref[...] = radial
+            eg[...] = terms
+        else:
+            rad_ref[...] += radial
+            eg[...] += terms
         grads[s, 0:rows, :] = mm(weights, img_u[...])
 
+    img_u[...] = img_f[...].T.astype(BF16)
     yh_copy.wait()
     ag_copy(1, 0, 1).start()
     ag_copy(1, 1, 1).start()
@@ -341,34 +351,41 @@
     rs_step(0, 1)
     rs_step(1, 1)
 
-    image_grad = eg[...]
-    unit_t = img_f[...]
-    radial = jnp.sum(unit_t * image_grad, axis=0, keepdims=True)
-    eg[...] = (image_grad - unit_t * radial) * inv_ref[...]
-    for j in range(TS):
-        theirs = pl.ds(pl.multiple_of(COLS * j + PIECE * (1 - c), 8), PIECE)
-        cx_s[j] = eg[theirs, :].astype(BF16)
-    cx_copy = rcopy(cx_s, cx_r, S_CX, S_CX, c_peer)
-    cx_copy.start()
-    rs_step(1, 2)
-    rs_step(0, 2)
-    cx_copy.wait()
-    for j in range(TS):
-        mine = pl.ds(pl.multiple_of(COLS * j + PIECE * c, 8), PIECE)
-        value = eg[mine, :] + cx_r[j].astype(F32)
-        px_f[j] = value
-        px_s[j] = value.astype(BF16)
-    exchange_start(px_s, px_r, S_PX)
+    radial = rad_ref[...]
+    inverse = inv_ref[...]
+
+    def emb_piece(j, half):
+        rows = pl.ds(pl.multiple_of(COLS * j + PIECE * half, 8), PIECE)
+        return (eg[rows, :] - img_f[rows, :] * radial) * inverse
+
+    def cx_copy(k):
+        j = tpeer(k)
+        return rcopy(cx_s.at[j], cx_r.at[j], S_CX + k % TS, S_CX + k % TS, c_peer)
+
+    for k in range(1, TS + 1):
+        cx_s[tpeer(k)] = emb_piece(tpeer(k), 1 - c).astype(BF16)
+        cx_copy(k).start()
+    for k in range(1, TS + 1):
+        j = tpeer(k)
+        value = emb_piece(j, c)
+        cx_copy(k).wait()
+        value = value + cx_r[j].astype(F32)
+        if k < TS:
+            px_s[j] = value.astype(BF16)
+            rcopy(px_s.at[j], px_r.at[t], S_PX + k, S_PX + t, (d, j)).start()
+        else:
+            px_f[...] = value
     px_r[t] = jnp.zeros((PIECE, IMGS), BF16)
-    rs_step(1, 3)
-    rs_step(0, 3)
-    rs_step(1, 4)
-    rs_step(0, 4)
+    emb_b[PIECE:WIDE, :] = jnp.zeros((WIDE - PIECE, IMGS), F32)
+    for s in range(2, 5):
+        rs_step(1, s)
+        rs_step(0, s)
     exchange_wait(px_s, px_r, S_PX)
-    emb_grad = px_f[t]
+    emb_grad = px_f[...]
     for j in range(TS):
         emb_grad = emb_grad + px_r[j].astype(F32)
-    vg_all[...] = mm(emb_grad.astype(BF16), feats[...]).T
+    emb_b[0:PIECE, :] = emb_grad
+    vg_all[...] = mm(emb_b[...].astype(BF16), feats[...]).T
 
     def vr_copy(way, s):
         sem = (S_VRP, S_VRM)[way] + s - 1
@@ -443,8 +460,19 @@
 
         @pl.when(q == k)
         def _():
-            vg_ref[:, 0:PIECE] = left[18 * k : 18 * (k + 1), :]
-            vg_ref[:, PIECE:COLS] = right[18 * k : 18 * (k + 1), :]
+            vg_ref[:, 0:PIECE] = left[18 * k : 18 * (k + 1), 0:PIECE]
+            vg_ref[:, PIECE:COLS] = right[18 * k : 18 * (k + 1), 0:PIECE]
+
+
+def hand_over(tg_in, vg_in, tg_out, vg_out, sem):
+    copies = [
+        pltpu.make_async_copy(tg_in, tg_out, sem.at[0]),
+        pltpu.make_async_copy(vg_in, vg_out, sem.at[1]),
+    ]
+    for copy in copies:
+        copy.start()
+    for copy in copies:
+        copy.wait()
 
 
 def local(
@@ -472,6 +500,7 @@
         ((E, IMGS), BF16),
         ((IMGS, E), BF16),
         ((1, IMGS), F32),
+        ((1, IMGS), F32),
         ((TS, TEXTS, D), BF16),
         ((TS, TEXTS, D), F32),
         ((TS, TEXTS, D), BF16),
@@ -491,15 +520,16 @@
         ((TEXTS, E), F32),
         ((TS, PIECE, IMGS), BF16),
         ((TS, PIECE, IMGS), BF16),
-        ((TS, PIECE, IMGS), F32),
+        ((PIECE, IMGS), F32),
         ((TS, PIECE, IMGS), BF16),
         ((TS, PIECE, IMGS), BF16),
-        ((D, PIECE), F32),
-        ((2, HALF, ZROWS, PIECE), F32),
-        ((2, HALF, ZROWS, PIECE), F32),
-        ((4, ZROWS, PIECE), F32),
+        ((WIDE, IMGS), F32),
+        ((D, WIDE), F32),
+        ((2, HALF, ZROWS, WIDE), F32),
+        ((2, HALF, ZROWS, WIDE), F32),
+        ((4, ZROWS, WIDE), F32),
     ]
-    return pl.pallas_call(
+    results = pl.pallas_call(
         kernel,
         out_shape=(
             jax.ShapeDtypeStruct((TEXTS, E), F32),
@@ -522,6 +552,14 @@
         image_features,
         vision_weight.T,
     )
+    return pl.pallas_call(
+        hand_over,
+        out_shape=tuple(jax.ShapeDtypeStruct(r.shape, F32) for r in results),
+        in_specs=[hbm] * 2,
+        out_specs=(hbm, hbm),
+        scratch_shapes=[pltpu.SemaphoreType.DMA((2,))],
+        compiler_params=pltpu.CompilerParams(vmem_limit_bytes=60 * 1024 * 1024),
+    )(*results)
 
 
 def solution(mesh):

time: 121 us -> 124 us (1.025)
  Pallas kernels: 117 us -> 123 us
  local copies, waits for them, and re-layouts: 2.9 us -> 0 us
    pallas_call x0 -> x1, Pallas kernels: none -> 5.22 us  [local(): pl.pallas_call(hand_over, out_shape=tuple((jax.ShapeDtypeStruct(r.shape,...]
    unnamed x2 -> x0, local copies, waits for them, and re-layouts: 2.9 us -> none
where the time goes in v3:
time: 124 us
  Pallas kernels  123 us (99%)
    pallas_call x1, Pallas kernels, local(): pl.pallas_call(kernel, out_shape=(jax.ShapeDtypeStruct((TEXTS, E), F32),...  118 us
    pallas_call x1, Pallas kernels, local(): pl.pallas_call(hand_over, out_shape=tuple((jax.ShapeDtypeStruct(r.shape,...  5.22 us

profile of v3, /device:TPU:1, one launch (start us, length us, event | category | flops | bytes accessed | tf_op | source)
XLA Modules:
  0.0 123.7 jit_solution(3417763812739006064)
XLA Ops:
  0.6 117.8 %shard_map.95 = (f32[20,1152]{1,0:T(8,128)}, f32[18,144]{1,0:T(8,128)}) custom-call(bf16[160,1152]{1,0:T(8,128)(2,1)} %text_ref.1, f32[1152]{0:T(1024)} %ln_ref.1, bf16[538,1152]{1,0:T(8,128)(2,1)} %bitcast.2, bf16[538,1152]{1,0:T(8,128)(2,1)} %down_ref.1, f32[1152]{0:T(1024)} %fg_ref.1, bf16[144,1152]{1,0:T(8,128)(2,1)} %head_ref.1, ...), custom_call_target="tpu_custom_call" | custom-call | tf_op jit(solution)/shard_map/pallas_call | solution.py:532
  118.5 5.2 %shard_map.96 = (f32[20,1152]{1,0:T(8,128)}, f32[18,144]{1,0:T(8,128)}) custom-call(f32[20,1152]{1,0:T(8,128)} %get-tuple-element.4.tg_in, f32[18,144]{1,0:T(8,128)} %get-tuple-element.5.vg_in), custom_call_target="tpu_custom_call" | custom-call | tf_op jit(solution)/shard_map/pallas_call | solution.py:555

commit v4 on v3

--- a/solution.py
+++ b/solution.py
@@ -53,8 +53,8 @@
 S_YH = S_HEAD + TS
 S_AG = S_YH + 1
 S_RS = S_AG + 4 * HALF
-S_YG = S_RS + 4 * HALF
-S_CX = S_YG + 1
+S_GY = S_RS + 2 * HALF
+S_CX = S_GY + 2 * HALF + 2
 S_PX = S_CX + TS
 S_VRP = S_PX + TS
 S_VRM = S_VRP + HALF
@@ -102,8 +102,8 @@
     eg,
     rs_s,
     rs_r,
-    yg_s,
-    yg_r,
+    gy_s,
+    gy_r,
     cx_s,
     cx_r,
     px_f,
@@ -260,8 +260,11 @@
     )
     texts[0, 0, 0] = text_unit.astype(BF16)
 
+    def is_first(s):
+        return isinstance(s, int) and s == 1
+
     def ag_copy(s, way, half):
-        source = texts.at[0, 0, half] if isinstance(s, int) and s == 1 else texts.at[s - 1, way, half]
+        source = texts.at[0, 0, half] if is_first(s) else texts.at[s - 1, way, half]
         sem = S_AG + 4 * (s - 1) + 2 * way + half
         return rcopy(source, texts.at[s, way, half], sem, sem, (z_next, z_prev)[way])
 
@@ -274,82 +277,99 @@
     col_ids = lax.broadcasted_iota(jnp.int32, (CHUNK, IMGS), 1)
     diagonal = ((row_ids < TEXTS) & (col_ids == row_ids + ROWS * c + TEXTS * t)).astype(F32)
 
-    def process(s, pieces):
+    def gy_copy(s, way):
+        sem = S_GY + 2 * s + way
+        return rcopy(gy_s.at[s, way], gy_r.at[s, way], sem, sem, yh_peer)
+
+    own_pieces = ((0, 0), (0, 1))
+    far_pieces = ((0, 0), (1, 1))
+    pair_pieces = ((0, 0), (0, 1), (1, 0), (1, 1))
+
+    def weigh(s, pieces):
         rows = TEXTS * len(pieces)
         for at, (way, half) in enumerate(pieces):
             block_f[TEXTS * at : TEXTS * (at + 1), :] = texts[s, way, half].astype(F32)
         block = block_f[0:rows, :].astype(BF16)
         dots = mm(block, img_ut[...])
         weights = jax.nn.sigmoid(logit_scale * dots + logit_bias)
-        if isinstance(s, int) and s == 0:
+        if pieces is own_pieces:
             weights = weights - diagonal
         weights = (weights * (logit_scale / ROWS)).astype(BF16)
         radial = jnp.sum(weights.astype(F32) * dots, axis=0, keepdims=True)
         terms = lax.dot_general(
             block, weights, (((0,), (0,)), ((), ())), preferred_element_type=F32
         )
-        if isinstance(s, int) and s == 0:
+        if pieces is own_pieces:
             rad_ref[...] = radial
             eg[...] = terms
         else:
             rad_ref[...] += radial
             eg[...] += terms
-        grads[s, 0:rows, :] = mm(weights, img_u[...])
-
-    img_u[...] = img_f[...].T.astype(BF16)
+        return weights
+
+    def text_terms(s, pieces, weights):
+        terms = mm(weights, img_u[...])
+        for at, (way, half) in enumerate(pieces):
+            part = terms[TEXTS * at : TEXTS * (at + 1)]
+            slot = way if pieces is pair_pieces else 0
+            if half == 0:
+                grads[s, slot] = part
+            else:
+                gy_s[s, slot] = part.astype(BF16)
+                gy_copy(s, slot).start()
+
+    def forward(s, half):
+        for way in range(2):
+            ag_copy(s, way, half).wait_recv()
+            if half == way:
+                ag_copy(s + 1, way, half).start()
+            else:
+
+                @pl.when(s < HALF - 1)
+                def _():
+                    ag_copy(s + 1, way, half).start()
+
     yh_copy.wait()
     ag_copy(1, 0, 1).start()
     ag_copy(1, 1, 1).start()
-    process(0, ((0, 0), (0, 1)))
+    img_u[...] = img_f[...].T.astype(BF16)
+    first_step = jnp.int32(1)
+    forward(first_step, 0)
+    own_weights = weigh(0, own_pieces)
+    forward(first_step, 1)
+    text_terms(0, own_pieces, own_weights)
 
     def ag_step(s, _):
-        for half in range(2):
-            for way in range(2):
-                ag_copy(s, way, half).wait_recv()
-                if half == way:
-                    ag_copy(s + 1, way, half).start()
-                else:
-
-                    @pl.when(s < HALF - 1)
-                    def _():
-                        ag_copy(s + 1, way, half).start()
-
-        process(s, ((0, 0), (0, 1), (1, 0), (1, 1)))
+        forward(s, 0)
+        weights = weigh(s - 1, pair_pieces)
+        forward(s, 1)
+        text_terms(s - 1, pair_pieces, weights)
         return 0
 
-    lax.fori_loop(1, HALF, ag_step, 0)
-
-    def rs_copy(way, s, half):
-        sem = S_RS + 4 * (s - 1) + 2 * way + half
-        return rcopy(
-            rs_s.at[way, s - 1, half], rs_r.at[way, s - 1, half], sem, sem, (z_next, z_prev)[way]
-        )
-
-    def rs_halves(way, s):
-        return (way,) if s == 1 else (1, 0)
+    lax.fori_loop(2, HALF, ag_step, 0)
+    text_terms(HALF - 1, pair_pieces, weigh(HALF - 1, pair_pieces))
+
+    def rs_copy(way, s):
+        sem = S_RS + 2 * (s - 1) + way
+        return rcopy(rs_s.at[way, s - 1], rs_r.at[way, s - 1], sem, sem, (z_next, z_prev)[way])
+
+    def rs_first(way):
+        return 1 + way
 
     def rs_step(way, s):
-        for half in rs_halves(way, s):
-            first = TEXTS * half if s == 1 else CHUNK * (1 - way) + TEXTS * half
-            value = grads[HALF + 1 - s, first : first + TEXTS, :]
-            if s > 1 and half in rs_halves(way, s - 1):
-                rs_copy(way, s - 1, half).wait_recv()
-                value = value + rs_r[way, s - 2, half].astype(F32)
-            rs_s[way, s - 1, half] = value.astype(BF16)
-            rs_copy(way, s, half).start()
-
-    def rs_last(half):
-        value = grads[0, TEXTS * half : TEXTS * (half + 1), :]
-        for way in range(2):
-            rs_copy(way, HALF, half).wait_recv()
-            value = value + rs_r[way, HALF - 1, half].astype(F32)
-        return value
+        left = HALF + 1 - s
+        slot = 0 if s == 1 else 1 - way
+        gy_copy(left, slot).wait_recv()
+        value = grads[left, slot] + gy_r[left, slot].astype(F32)
+        if s > rs_first(way):
+            rs_copy(way, s - 1).wait_recv()
+            value = value + rs_r[way, s - 2].astype(F32)
+        rs_s[way, s - 1] = value.astype(BF16)
+        rs_copy(way, s).start()
 
     ag_copy(HALF, 0, 0).wait_recv()
     ag_copy(HALF, 1, 1).wait_recv()
-    process(HALF, ((0, 0), (1, 1)))
-    rs_step(0, 1)
-    rs_step(1, 1)
+    text_terms(HALF, far_pieces, weigh(HALF, far_pieces))
 
     radial = rad_ref[...]
     inverse = inv_ref[...]
@@ -365,6 +385,8 @@
     for k in range(1, TS + 1):
         cx_s[tpeer(k)] = emb_piece(tpeer(k), 1 - c).astype(BF16)
         cx_copy(k).start()
+    rs_step(0, 1)
+    rs_step(1, 2)
     for k in range(1, TS + 1):
         j = tpeer(k)
         value = emb_piece(j, c)
@@ -377,9 +399,9 @@
             px_f[...] = value
     px_r[t] = jnp.zeros((PIECE, IMGS), BF16)
     emb_b[PIECE:WIDE, :] = jnp.zeros((WIDE - PIECE, IMGS), F32)
-    for s in range(2, 5):
-        rs_step(1, s)
+    for s in range(2, 4):
         rs_step(0, s)
+        rs_step(1, s + 1)
     exchange_wait(px_s, px_r, S_PX)
     emb_grad = px_f[...]
     for j in range(TS):
@@ -407,17 +429,20 @@
         vr_step(0, s)
         if s < HALF:
             vr_step(1, s)
-        r = s + 4
-        if r <= HALF:
-            rs_step(1, r)
-            rs_step(0, r)
-        if r == HALF + 1:
-            yg_s[...] = rs_last(1)
-            rcopy(yg_s, yg_r, S_YG, S_YG, yh_peer).start()
-
-    own_grad = rs_last(0)
-    rcopy(yg_s, yg_r, S_YG, S_YG, yh_peer).wait()
-    tg_ref[...] = own_grad + yg_r[...]
+        if s + 3 <= HALF:
+            rs_step(0, s + 3)
+        if s + 4 <= HALF:
+            rs_step(1, s + 4)
+        if s == HALF - 2:
+            gy_copy(0, 0).wait_recv()
+            rs_copy(0, HALF).wait_recv()
+            rs_copy(1, HALF).wait_recv()
+            tg_ref[...] = (
+                grads[0, 0]
+                + gy_r[0, 0].astype(F32)
+                + rs_r[0, HALF - 1].astype(F32)
+                + rs_r[1, HALF - 1].astype(F32)
+            )
 
     vr_copy(0, HALF).wait_recv()
     vr_copy(1, HALF - 1).wait_recv()
@@ -443,10 +468,19 @@
         return 0
 
     lax.fori_loop(2, HALF + 1, ag_drain, 0)
+
+    def gy_drain(s, _):
+        gy_copy(s, 0).wait_send()
+        gy_copy(s, 1).wait_send()
+        return 0
+
+    gy_copy(0, 0).wait_send()
+    lax.fori_loop(1, HALF, gy_drain, 0)
+    gy_copy(HALF, 0).wait_send()
     for s in range(1, HALF + 1):
         for way in range(2):
-            for half in rs_halves(way, s):
-                rs_copy(way, s, half).wait_send()
+            if s >= rs_first(way):
+                rs_copy(way, s).wait_send()
             if s < HALF or way == 0:
                 vr_copy(way, s).wait_send()
 
@@ -462,17 +496,6 @@
         def _():
             vg_ref[:, 0:PIECE] = left[18 * k : 18 * (k + 1), 0:PIECE]
             vg_ref[:, PIECE:COLS] = right[18 * k : 18 * (k + 1), 0:PIECE]
-
-
-def hand_over(tg_in, vg_in, tg_out, vg_out, sem):
-    copies = [
-        pltpu.make_async_copy(tg_in, tg_out, sem.at[0]),
-        pltpu.make_async_copy(vg_in, vg_out, sem.at[1]),
-    ]
-    for copy in copies:
-        copy.start()
-    for copy in copies:
-        copy.wait()
 
 
 def local(
@@ -512,12 +535,12 @@
         ((TS, TEXTS, E), BF16),
         ((2 * CHUNK, E), F32),
         ((HALF + 1, 2, 2, TEXTS, E), BF16),
-        ((HALF + 1, 2 * CHUNK, E), F32),
+        ((HALF + 1, 2, TEXTS, E), F32),
         ((E, IMGS), F32),
-        ((2, HALF, 2, TEXTS, E), BF16),
-        ((2, HALF, 2, TEXTS, E), BF16),
-        ((TEXTS, E), F32),
-        ((TEXTS, E), F32),
+        ((2, HALF, TEXTS, E), BF16),
+        ((2, HALF, TEXTS, E), BF16),
+        ((HALF + 1, 2, TEXTS, E), BF16),
+        ((HALF + 1, 2, TEXTS, E), BF16),
         ((TS, PIECE, IMGS), BF16),
         ((TS, PIECE, IMGS), BF16),
         ((PIECE, IMGS), F32),
@@ -529,7 +552,7 @@
         ((2, HALF, ZROWS, WIDE), F32),
         ((4, ZROWS, WIDE), F32),
     ]
-    results = pl.pallas_call(
+    return pl.pallas_call(
         kernel,
         out_shape=(
             jax.ShapeDtypeStruct((TEXTS, E), F32),
@@ -552,14 +575,6 @@
         image_features,
         vision_weight.T,
     )
-    return pl.pallas_call(
-        hand_over,
-        out_shape=tuple(jax.ShapeDtypeStruct(r.shape, F32) for r in results),
-        in_specs=[hbm] * 2,
-        out_specs=(hbm, hbm),
-        scratch_shapes=[pltpu.SemaphoreType.DMA((2,))],
-        compiler_params=pltpu.CompilerParams(vmem_limit_bytes=60 * 1024 * 1024),
-    )(*results)
 
 
 def solution(mesh):

time: 124 us -> 120 us (0.968)
  Pallas kernels: 123 us -> 116 us
  local copies, waits for them, and re-layouts: 0 us -> 2.9 us
    pallas_call x1 -> x0, Pallas kernels: 5.22 us -> none  [local(): pl.pallas_call(hand_over, out_shape=tuple((jax.ShapeDtypeStruct(r.shape,...]
    unnamed x0 -> x2, local copies, waits for them, and re-layouts: none -> 2.9 us
    pallas_call x1, Pallas kernels: 118 us -> 116 us  [local(): pl.pallas_call(kernel, out_shape=(jax.ShapeDtypeStruct((TEXTS, E), F32),...]
where the time goes in v4:
time: 120 us
  Pallas kernels  116 us (97%)
  local copies, waits for them, and re-layouts  2.9 us (2%)
    pallas_call x1, Pallas kernels, local(): pl.pallas_call(kernel, out_shape=(jax.ShapeDtypeStruct((TEXTS, E), F32),...  116 us
    unnamed x2, local copies, waits for them, and re-layouts  2.9 us

profile of v4, /device:TPU:1, one launch (start us, length us, event | category | flops | bytes accessed | tf_op | source)
XLA Modules:
  0.0 119.6 jit_solution(13941804680495629387)
XLA Ops:
  0.6 116.1 %shard_map.95 = (f32[20,1152]{1,0:T(8,128)}, f32[18,144]{1,0:T(8,128)}) custom-call(bf16[160,1152]{1,0:T(8,128)(2,1)} %text_ref.1, f32[1152]{0:T(1024)} %ln_ref.1, bf16[538,1152]{1,0:T(8,128)(2,1)} %bitcast.2, bf16[538,1152]{1,0:T(8,128)(2,1)} %down_ref.1, f32[1152]{0:T(1024)} %fg_ref.1, bf16[144,1152]{1,0:T(8,128)(2,1)} %head_ref.1, ...), custom_call_target="tpu_custom_call" | custom-call | tf_op jit(solution)/shard_map/pallas_call | solution.py:555
  116.7 1.5 %copy.12 = f32[20,1152]{1,0:T(8,128)} copy(f32[20,1152]{1,0:T(8,128)} %get-tuple-element.4) | data formatting | bytes 184320
  118.3 1.3 %copy.13 = f32[18,144]{1,0:T(8,128)} copy(f32[18,144]{1,0:T(8,128)} %get-tuple-element.5) | data formatting | bytes 20736

commit v5 on v4

--- a/solution.py
+++ b/solution.py
@@ -56,9 +56,8 @@
 S_GY = S_RS + 2 * HALF
 S_CX = S_GY + 2 * HALF + 2
 S_PX = S_CX + TS
-S_VRP = S_PX + TS
-S_VRM = S_VRP + HALF
-S_FX = S_VRM + HALF
+S_VR = S_PX + TS
+S_FX = S_VR + ZS
 S_ALL = S_FX + 4
 L_FEAT, L_UP, L_DOWN, L_HEAD, L_VIS = range(5)
 
@@ -97,8 +96,14 @@
     head_f,
     head_r,
     block_f,
+    ends_f,
     texts,
     grads,
+    w_pad,
+    w_ends,
+    wt_all,
+    text_all,
+    eg_n,
     eg,
     rs_s,
     rs_r,
@@ -147,7 +152,8 @@
         )
 
     barrier = pltpu.get_barrier_semaphore()
-    greeted = [z_next, z_prev] + [(d, tpeer(k)) for k in range(1, TS)]
+    z_peers = [(lax.rem(z + k, ZS) * 4 + base, t) for k in range(1, ZS)]
+    greeted = z_peers + [(d, tpeer(k)) for k in range(1, TS)]
     fx_peers = [(4 * z + lax.rem(q + k, 4), t) for k in range(1, 4)]
     greeted = greeted + fx_peers
     for dev in greeted:
@@ -156,6 +162,9 @@
     own_rows = pl.ds(pl.multiple_of(ROWS * c, 32), ROWS)
     other_rows = pl.ds(pl.multiple_of(ROWS * (1 - c), 32), ROWS)
     feats[2 * ROWS : IMGS, :] = jnp.zeros((IMGS - 2 * ROWS, D), BF16)
+    w_pad[2 * CHUNK : WIDE, :] = jnp.zeros((WIDE - 2 * CHUNK, IMGS), F32)
+    w_ends[2 * CHUNK : WIDE, :] = jnp.zeros((WIDE - 2 * CHUNK, IMGS), F32)
+    text_all[...] = jnp.zeros_like(text_all)
     loads = [
         pltpu.make_async_copy(src, dst, load_sem.at[at])
         for at, (src, dst) in enumerate(
@@ -287,25 +296,34 @@
 
     def weigh(s, pieces):
         rows = TEXTS * len(pieces)
+        first = CHUNK if pieces is far_pieces else 0
+        rows_f = block_f if pieces is pair_pieces else ends_f
+        weights_f = w_pad if pieces is pair_pieces else w_ends
         for at, (way, half) in enumerate(pieces):
-            block_f[TEXTS * at : TEXTS * (at + 1), :] = texts[s, way, half].astype(F32)
-        block = block_f[0:rows, :].astype(BF16)
+            rows_f[first + TEXTS * at : first + TEXTS * (at + 1), :] = texts[s, way, half].astype(F32)
+        block = rows_f[first : first + rows, :].astype(BF16)
         dots = mm(block, img_ut[...])
         weights = jax.nn.sigmoid(logit_scale * dots + logit_bias)
         if pieces is own_pieces:
             weights = weights - diagonal
         weights = (weights * (logit_scale / ROWS)).astype(BF16)
-        radial = jnp.sum(weights.astype(F32) * dots, axis=0, keepdims=True)
-        terms = lax.dot_general(
-            block, weights, (((0,), (0,)), ((), ())), preferred_element_type=F32
-        )
+        wide_weights = weights.astype(F32)
+        radial = jnp.sum(wide_weights * dots, axis=0, keepdims=True)
+        weights_f[first : first + rows, :] = wide_weights
         if pieces is own_pieces:
             rad_ref[...] = radial
-            eg[...] = terms
         else:
             rad_ref[...] += radial
-            eg[...] += terms
+        if pieces is pair_pieces:
+            keep(s - 1, block_f, w_pad)
         return weights
+
+    def keep(place, rows_f, weights_f):
+        at = WIDE * place
+        if not isinstance(place, int):
+            at = pl.multiple_of(at, WIDE)
+        text_all[pl.ds(at, 2 * CHUNK), :] = rows_f[...].astype(BF16)
+        wt_all[:, pl.ds(at, WIDE)] = weights_f[...].T.astype(BF16)
 
     def text_terms(s, pieces, weights):
         terms = mm(weights, img_u[...])
@@ -348,6 +366,8 @@
 
     lax.fori_loop(2, HALF, ag_step, 0)
     text_terms(HALF - 1, pair_pieces, weigh(HALF - 1, pair_pieces))
+    most = WIDE * (HALF - 1)
+    eg_n[...] = mm(wt_all[:, 0:most], text_all[0:most, :])
 
     def rs_copy(way, s):
         sem = S_RS + 2 * (s - 1) + way
@@ -369,7 +389,9 @@
 
     ag_copy(HALF, 0, 0).wait_recv()
     ag_copy(HALF, 1, 1).wait_recv()
-    text_terms(HALF, far_pieces, weigh(HALF, far_pieces))
+    far_weights = weigh(HALF, far_pieces)
+    keep(HALF - 1, ends_f, w_ends)
+    eg[...] = (eg_n[...] + mm(wt_all[:, most:], text_all[most:, :])).T
 
     radial = rad_ref[...]
     inverse = inv_ref[...]
@@ -385,7 +407,7 @@
     for k in range(1, TS + 1):
         cx_s[tpeer(k)] = emb_piece(tpeer(k), 1 - c).astype(BF16)
         cx_copy(k).start()
-    rs_step(0, 1)
+    text_terms(HALF, far_pieces, far_weights)
     rs_step(1, 2)
     for k in range(1, TS + 1):
         j = tpeer(k)
@@ -399,6 +421,7 @@
             px_f[...] = value
     px_r[t] = jnp.zeros((PIECE, IMGS), BF16)
     emb_b[PIECE:WIDE, :] = jnp.zeros((WIDE - PIECE, IMGS), F32)
+    rs_step(0, 1)
     for s in range(2, 4):
         rs_step(0, s)
         rs_step(1, s + 1)
@@ -409,44 +432,42 @@
     emb_b[0:PIECE, :] = emb_grad
     vg_all[...] = mm(emb_b[...].astype(BF16), feats[...]).T
 
-    def vr_copy(way, s):
-        sem = (S_VRP, S_VRM)[way] + s - 1
-        return rcopy(vr_s.at[way, s - 1], vr_r.at[way, s - 1], sem, sem, (z_next, z_prev)[way])
-
-    def vg_chunk(owner):
-        return vg_all[pl.ds(pl.multiple_of(ZROWS * owner, 8), ZROWS), :]
-
-    def vr_step(way, s):
-        owner = zmod(z + HALF + 1 - s) if way == 0 else zmod(z - HALF + s)
-        value = vg_chunk(owner)
-        if s > 1:
-            vr_copy(way, s - 1).wait_recv()
-            value = value + vr_r[way, s - 2]
-        vr_s[way, s - 1] = value
-        vr_copy(way, s).start()
-
-    for s in range(1, HALF + 1):
-        vr_step(0, s)
+    def vr_copy(k):
+        o = zmod(z + k)
+        return rcopy(vr_s.at[o], vr_r.at[z], S_VR + k, S_VR + z, z_peers[k - 1])
+
+    def vr_in(k):
+        o = zmod(z + k)
+        return rcopy(vr_s.at[o], vr_r.at[o], S_VR + k, S_VR + o, z_peers[k - 1])
+
+    for o in range(ZS):
+        vr_s[o] = vg_all[ZROWS * o : ZROWS * (o + 1), 0:PIECE].astype(BF16)
+    far_first = sorted(range(1, ZS), key=lambda k: -min(k, ZS - k))
+    for k in far_first:
+        vr_copy(k).start()
+    vr_r[z] = jnp.zeros((ZROWS, PIECE), BF16)
+
+    for s in range(4, HALF + 1):
+        rs_step(0, s)
         if s < HALF:
-            vr_step(1, s)
-        if s + 3 <= HALF:
-            rs_step(0, s + 3)
-        if s + 4 <= HALF:
-            rs_step(1, s + 4)
-        if s == HALF - 2:
-            gy_copy(0, 0).wait_recv()
-            rs_copy(0, HALF).wait_recv()
-            rs_copy(1, HALF).wait_recv()
-            tg_ref[...] = (
-                grads[0, 0]
-                + gy_r[0, 0].astype(F32)
-                + rs_r[0, HALF - 1].astype(F32)
-                + rs_r[1, HALF - 1].astype(F32)
-            )
-
-    vr_copy(0, HALF).wait_recv()
-    vr_copy(1, HALF - 1).wait_recv()
-    fx[q] = vg_chunk(z) + vr_r[0, HALF - 1] + vr_r[1, HALF - 2]
+            rs_step(1, s + 1)
+    gy_copy(0, 0).wait_recv()
+    rs_copy(0, HALF).wait_recv()
+    rs_copy(1, HALF).wait_recv()
+    tg_ref[...] = (
+        grads[0, 0]
+        + gy_r[0, 0].astype(F32)
+        + rs_r[0, HALF - 1].astype(F32)
+        + rs_r[1, HALF - 1].astype(F32)
+    )
+
+    total_vg = vg_all[pl.ds(pl.multiple_of(ZROWS * z, 8), ZROWS), :][:, 0:PIECE]
+    for k in far_first:
+        vr_copy(k).wait_send()
+        vr_in(k).wait_recv()
+    for o in range(ZS):
+        total_vg = total_vg + vr_r[o].astype(F32)
+    fx[q] = total_vg
     for k in range(1, 4):
         rcopy(fx.at[q], fx.at[q], S_FX + k, S_FX + q, fx_peers[k - 1]).start()
 
@@ -481,8 +502,6 @@
         for way in range(2):
             if s >= rs_first(way):
                 rs_copy(way, s).wait_send()
-            if s < HALF or way == 0:
-                vr_copy(way, s).wait_send()
 
     for k in range(1, 4):
         o = lax.rem(q + k, 4)
@@ -534,8 +553,14 @@
         ((TS, TEXTS, E), F32),
         ((TS, TEXTS, E), BF16),
         ((2 * CHUNK, E), F32),
+        ((2 * CHUNK, E), F32),
         ((HALF + 1, 2, 2, TEXTS, E), BF16),
         ((HALF + 1, 2, TEXTS, E), F32),
+        ((WIDE, IMGS), F32),
+        ((WIDE, IMGS), F32),
+        ((IMGS, HALF * WIDE), BF16),
+        ((HALF * WIDE, E), BF16),
+        ((IMGS, E), F32),
         ((E, IMGS), F32),
         ((2, HALF, TEXTS, E), BF16),
         ((2, HALF, TEXTS, E), BF16),
@@ -548,9 +573,9 @@
         ((TS, PIECE, IMGS), BF16),
         ((WIDE, IMGS), F32),
         ((D, WIDE), F32),
-        ((2, HALF, ZROWS, WIDE), F32),
-        ((2, HALF, ZROWS, WIDE), F32),
-        ((4, ZROWS, WIDE), F32),
+        ((ZS, ZROWS, PIECE), BF16),
+        ((ZS, ZROWS, PIECE), BF16),
+        ((4, ZROWS, PIECE), F32),
     ]
     return pl.pallas_call(
         kernel,

time: 120 us -> 124 us (1.033)
  Pallas kernels: 116 us -> 119 us
    pallas_call x1, Pallas kernels: 116 us -> 119 us  [local(): pl.pallas_call(kernel, out_shape=(jax.ShapeDtypeStruct((TEXTS, E), F32),...]
where the time goes in v5:
time: 124 us; the launch traced here: 123 us
  Pallas kernels  119 us (96%)
  local copies, waits for them, and re-layouts  2.9 us (2%)
    pallas_call x1, Pallas kernels, local(): pl.pallas_call(kernel, out_shape=(jax.ShapeDtypeStruct((TEXTS, E), F32),...  119 us
    unnamed x2, local copies, waits for them, and re-layouts  2.9 us

profile of v5, /device:TPU:1, one launch (start us, length us, event | category | flops | bytes accessed | tf_op | source)
XLA Modules:
  0.0 122.6 jit_solution(5294316470591830423)
XLA Ops:
  0.6 119.1 %shard_map.95 = (f32[20,1152]{1,0:T(8,128)}, f32[18,144]{1,0:T(8,128)}) custom-call(bf16[160,1152]{1,0:T(8,128)(2,1)} %text_ref.1, f32[1152]{0:T(1024)} %ln_ref.1, bf16[538,1152]{1,0:T(8,128)(2,1)} %bitcast.2, bf16[538,1152]{1,0:T(8,128)(2,1)} %down_ref.1, f32[1152]{0:T(1024)} %fg_ref.1, bf16[144,1152]{1,0:T(8,128)(2,1)} %head_ref.1, ...), custom_call_target="tpu_custom_call" | custom-call | tf_op jit(solution)/shard_map/pallas_call | solution.py:580
  119.7 1.5 %copy.12 = f32[20,1152]{1,0:T(8,128)} copy(f32[20,1152]{1,0:T(8,128)} %get-tuple-element.4) | data formatting | bytes 184320
  121.3 1.3 %copy.13 = f32[18,144]{1,0:T(8,128)} copy(f32[18,144]{1,0:T(8,128)} %get-tuple-element.5) | data formatting | bytes 20736

commit v6 on v5

--- a/solution.py
+++ b/solution.py
@@ -96,14 +96,8 @@
     head_f,
     head_r,
     block_f,
-    ends_f,
     texts,
     grads,
-    w_pad,
-    w_ends,
-    wt_all,
-    text_all,
-    eg_n,
     eg,
     rs_s,
     rs_r,
@@ -162,9 +156,6 @@
     own_rows = pl.ds(pl.multiple_of(ROWS * c, 32), ROWS)
     other_rows = pl.ds(pl.multiple_of(ROWS * (1 - c), 32), ROWS)
     feats[2 * ROWS : IMGS, :] = jnp.zeros((IMGS - 2 * ROWS, D), BF16)
-    w_pad[2 * CHUNK : WIDE, :] = jnp.zeros((WIDE - 2 * CHUNK, IMGS), F32)
-    w_ends[2 * CHUNK : WIDE, :] = jnp.zeros((WIDE - 2 * CHUNK, IMGS), F32)
-    text_all[...] = jnp.zeros_like(text_all)
     loads = [
         pltpu.make_async_copy(src, dst, load_sem.at[at])
         for at, (src, dst) in enumerate(
@@ -296,34 +287,25 @@
 
     def weigh(s, pieces):
         rows = TEXTS * len(pieces)
-        first = CHUNK if pieces is far_pieces else 0
-        rows_f = block_f if pieces is pair_pieces else ends_f
-        weights_f = w_pad if pieces is pair_pieces else w_ends
         for at, (way, half) in enumerate(pieces):
-            rows_f[first + TEXTS * at : first + TEXTS * (at + 1), :] = texts[s, way, half].astype(F32)
-        block = rows_f[first : first + rows, :].astype(BF16)
+            block_f[TEXTS * at : TEXTS * (at + 1), :] = texts[s, way, half].astype(F32)
+        block = block_f[0:rows, :].astype(BF16)
         dots = mm(block, img_ut[...])
         weights = jax.nn.sigmoid(logit_scale * dots + logit_bias)
         if pieces is own_pieces:
             weights = weights - diagonal
         weights = (weights * (logit_scale / ROWS)).astype(BF16)
-        wide_weights = weights.astype(F32)
-        radial = jnp.sum(wide_weights * dots, axis=0, keepdims=True)
-        weights_f[first : first + rows, :] = wide_weights
+        radial = jnp.sum(weights.astype(F32) * dots, axis=0, keepdims=True)
+        terms = lax.dot_general(
+            block, weights, (((0,), (0,)), ((), ())), preferred_element_type=F32
+        )
         if pieces is own_pieces:
             rad_ref[...] = radial
+            eg[...] = terms
         else:
             rad_ref[...] += radial
-        if pieces is pair_pieces:
-            keep(s - 1, block_f, w_pad)
+            eg[...] += terms
         return weights
-
-    def keep(place, rows_f, weights_f):
-        at = WIDE * place
-        if not isinstance(place, int):
-            at = pl.multiple_of(at, WIDE)
-        text_all[pl.ds(at, 2 * CHUNK), :] = rows_f[...].astype(BF16)
-        wt_all[:, pl.ds(at, WIDE)] = weights_f[...].T.astype(BF16)
 
     def text_terms(s, pieces, weights):
         terms = mm(weights, img_u[...])
@@ -366,8 +348,6 @@
 
     lax.fori_loop(2, HALF, ag_step, 0)
     text_terms(HALF - 1, pair_pieces, weigh(HALF - 1, pair_pieces))
-    most = WIDE * (HALF - 1)
-    eg_n[...] = mm(wt_all[:, 0:most], text_all[0:most, :])
 
     def rs_copy(way, s):
         sem = S_RS + 2 * (s - 1) + way
@@ -390,8 +370,6 @@
     ag_copy(HALF, 0, 0).wait_recv()
     ag_copy(HALF, 1, 1).wait_recv()
     far_weights = weigh(HALF, far_pieces)
-    keep(HALF - 1, ends_f, w_ends)
-    eg[...] = (eg_n[...] + mm(wt_all[:, most:], text_all[most:, :])).T
 
     radial = rad_ref[...]
     inverse = inv_ref[...]
@@ -553,14 +531,8 @@
         ((TS, TEXTS, E), F32),
         ((TS, TEXTS, E), BF16),
         ((2 * CHUNK, E), F32),
-        ((2 * CHUNK, E), F32),
         ((HALF + 1, 2, 2, TEXTS, E), BF16),
         ((HALF + 1, 2, TEXTS, E), F32),
-        ((WIDE, IMGS), F32),
-        ((WIDE, IMGS), F32),
-        ((IMGS, HALF * WIDE), BF16),
-        ((HALF * WIDE, E), BF16),
-        ((IMGS, E), F32),
         ((E, IMGS), F32),
         ((2, HALF, TEXTS, E), BF16),
         ((2, HALF, TEXTS, E), BF16),

time: 124 us -> 124 us (level)
  no operation moved by 1% of the time
where the time goes in v6:
time: 124 us; the launch traced here: 122 us
  Pallas kernels  119 us (96%)
  local copies, waits for them, and re-layouts  2.9 us (2%)
    pallas_call x1, Pallas kernels, local(): pl.pallas_call(kernel, out_shape=(jax.ShapeDtypeStruct((TEXTS, E), F32),...  119 us
    unnamed x2, local copies, waits for them, and re-layouts  2.9 us

profile of v6, /device:TPU:1, one launch (start us, length us, event | category | flops | bytes accessed | tf_op | source)
XLA Modules:
  0.0 122.2 jit_solution(24880785865166226)
XLA Ops:
  0.6 118.7 %shard_map.95 = (f32[20,1152]{1,0:T(8,128)}, f32[18,144]{1,0:T(8,128)}) custom-call(bf16[160,1152]{1,0:T(8,128)(2,1)} %text_ref.1, f32[1152]{0:T(1024)} %ln_ref.1, bf16[538,1152]{1,0:T(8,128)(2,1)} %bitcast.2, bf16[538,1152]{1,0:T(8,128)(2,1)} %down_ref.1, f32[1152]{0:T(1024)} %fg_ref.1, bf16[144,1152]{1,0:T(8,128)(2,1)} %head_ref.1, ...), custom_call_target="tpu_custom_call" | custom-call | tf_op jit(solution)/shard_map/pallas_call | solution.py:552
  119.3 1.5 %copy.12 = f32[20,1152]{1,0:T(8,128)} copy(f32[20,1152]{1,0:T(8,128)} %get-tuple-element.4) | data formatting | bytes 184320
  120.9 1.3 %copy.13 = f32[18,144]{1,0:T(8,128)} copy(f32[18,144]{1,0:T(8,128)} %get-tuple-element.5) | data formatting | bytes 20736

commit v7 on v4

--- a/solution.py
+++ b/solution.py
@@ -54,7 +54,8 @@
 S_AG = S_YH + 1
 S_RS = S_AG + 4 * HALF
 S_GY = S_RS + 2 * HALF
-S_CX = S_GY + 2 * HALF + 2
+S_FAR = S_GY + 2 * HALF + 2
+S_CX = S_FAR + 1
 S_PX = S_CX + TS
 S_VRP = S_PX + TS
 S_VRM = S_VRP + HALF
@@ -104,6 +105,8 @@
     rs_r,
     gy_s,
     gy_r,
+    far_s,
+    far_r,
     cx_s,
     cx_r,
     px_f,
@@ -147,7 +150,8 @@
         )
 
     barrier = pltpu.get_barrier_semaphore()
-    greeted = [z_next, z_prev] + [(d, tpeer(k)) for k in range(1, TS)]
+    z_far = (lax.rem(z + HALF, ZS) * 4 + base, t)
+    greeted = [z_next, z_prev, z_far] + [(d, tpeer(k)) for k in range(1, TS)]
     fx_peers = [(4 * z + lax.rem(q + k, 4), t) for k in range(1, 4)]
     greeted = greeted + fx_peers
     for dev in greeted:
@@ -205,11 +209,13 @@
     feat_copy.wait_send()
     rcopy(feats.at[other_rows], feats.at[other_rows], S_FEAT, S_FEAT, c_peer).wait_recv()
     part_t[...] = mm_t(vis_v[...], feats[...])
-    img_s[...] = part_t[pl.ds(pl.multiple_of(PIECE * c, 8), PIECE), :].astype(BF16)
+    img_s[...] = part_t[pl.ds(pl.multiple_of(PIECE * c, 8), PIECE), :][:, 0 : 2 * ROWS].astype(BF16)
     for k in range(1, TS):
         rcopy(img_s, img_r.at[c, t], S_IMG + k, S_IMG + t, (d, tpeer(k))).start()
     img_r[c, t] = img_s[...]
 
+    img_f[:, 2 * WIDE : IMGS] = jnp.zeros((E, IMGS - 2 * WIDE), F32)
+    emb_b[...] = jnp.zeros_like(emb_b)
     exchange_wait(mix_s, mix_r, S_MIX)
     total = mix_f[t]
     for j in range(TS):
@@ -243,7 +249,7 @@
     for j in range(TS):
         for h in range(2):
             at = COLS * j + PIECE * h
-            img_f[at : at + PIECE, :] = img_r[h, j].astype(F32)
+            img_f[at : at + PIECE, 0 : 2 * ROWS] = img_r[h, j].astype(F32)
     emb_t = img_f[...]
     inverse = lax.rsqrt(jnp.sum(emb_t * emb_t, axis=0, keepdims=True) + norm_eps)
     inv_ref[...] = inverse
@@ -353,30 +359,31 @@
         sem = S_RS + 2 * (s - 1) + way
         return rcopy(rs_s.at[way, s - 1], rs_r.at[way, s - 1], sem, sem, (z_next, z_prev)[way])
 
-    def rs_first(way):
-        return 1 + way
-
-    def rs_step(way, s):
+    def rs_step(s):
         left = HALF + 1 - s
-        slot = 0 if s == 1 else 1 - way
-        gy_copy(left, slot).wait_recv()
-        value = grads[left, slot] + gy_r[left, slot].astype(F32)
-        if s > rs_first(way):
-            rs_copy(way, s - 1).wait_recv()
-            value = value + rs_r[way, s - 2].astype(F32)
-        rs_s[way, s - 1] = value.astype(BF16)
-        rs_copy(way, s).start()
-
+        for way in range(2):
+            slot = 1 - way
+            gy_copy(left, slot).wait_recv()
+            value = grads[left, slot] + gy_r[left, slot].astype(F32)
+            if s > 2:
+                rs_copy(way, s - 1).wait_recv()
+                value = value + rs_r[way, s - 2].astype(F32)
+            rs_s[way, s - 1] = value.astype(BF16)
+            rs_copy(way, s).start()
+
+    far_copy = rcopy(far_s, far_r, S_FAR, S_FAR, z_far)
+
+    rs_step(2)
     ag_copy(HALF, 0, 0).wait_recv()
     ag_copy(HALF, 1, 1).wait_recv()
-    text_terms(HALF, far_pieces, weigh(HALF, far_pieces))
+    far_weights = weigh(HALF, far_pieces)
 
     radial = rad_ref[...]
     inverse = inv_ref[...]
 
     def emb_piece(j, half):
         rows = pl.ds(pl.multiple_of(COLS * j + PIECE * half, 8), PIECE)
-        return (eg[rows, :] - img_f[rows, :] * radial) * inverse
+        return ((eg[rows, :] - img_f[rows, :] * radial) * inverse)[:, 0 : 2 * ROWS]
 
     def cx_copy(k):
         j = tpeer(k)
@@ -385,8 +392,7 @@
     for k in range(1, TS + 1):
         cx_s[tpeer(k)] = emb_piece(tpeer(k), 1 - c).astype(BF16)
         cx_copy(k).start()
-    rs_step(0, 1)
-    rs_step(1, 2)
+    text_terms(HALF, far_pieces, far_weights)
     for k in range(1, TS + 1):
         j = tpeer(k)
         value = emb_piece(j, c)
@@ -397,16 +403,18 @@
             rcopy(px_s.at[j], px_r.at[t], S_PX + k, S_PX + t, (d, j)).start()
         else:
             px_f[...] = value
-    px_r[t] = jnp.zeros((PIECE, IMGS), BF16)
-    emb_b[PIECE:WIDE, :] = jnp.zeros((WIDE - PIECE, IMGS), F32)
-    for s in range(2, 4):
-        rs_step(0, s)
-        rs_step(1, s + 1)
+    px_r[t] = jnp.zeros((PIECE, 2 * ROWS), BF16)
+    rs_step(3)
+    gy_copy(HALF, 0).wait_recv()
+    far_s[...] = (grads[HALF, 0] + gy_r[HALF, 0].astype(F32)).astype(BF16)
+    far_copy.start()
+    rs_step(4)
+    rs_step(5)
     exchange_wait(px_s, px_r, S_PX)
     emb_grad = px_f[...]
     for j in range(TS):
         emb_grad = emb_grad + px_r[j].astype(F32)
-    emb_b[0:PIECE, :] = emb_grad
+    emb_b[0:PIECE, 0 : 2 * ROWS] = emb_grad
     vg_all[...] = mm(emb_b[...].astype(BF16), feats[...]).T
 
     def vr_copy(way, s):
@@ -414,7 +422,7 @@
         return rcopy(vr_s.at[way, s - 1], vr_r.at[way, s - 1], sem, sem, (z_next, z_prev)[way])
 
     def vg_chunk(owner):
-        return vg_all[pl.ds(pl.multiple_of(ZROWS * owner, 8), ZROWS), :]
+        return vg_all[pl.ds(pl.multiple_of(ZROWS * owner, 8), ZROWS), :][:, 0:PIECE]
 
     def vr_step(way, s):
         owner = zmod(z + HALF + 1 - s) if way == 0 else zmod(z - HALF + s)
@@ -429,11 +437,10 @@
         vr_step(0, s)
         if s < HALF:
             vr_step(1, s)
-        if s + 3 <= HALF:
-            rs_step(0, s + 3)
-        if s + 4 <= HALF:
-            rs_step(1, s + 4)
-        if s == HALF - 2:
+        if s + 5 <= HALF:
+            rs_step(s + 5)
+        if s == HALF - 3:
+            far_copy.wait()
             gy_copy(0, 0).wait_recv()
             rs_copy(0, HALF).wait_recv()
             rs_copy(1, HALF).wait_recv()
@@ -442,6 +449,7 @@
                 + gy_r[0, 0].astype(F32)
                 + rs_r[0, HALF - 1].astype(F32)
                 + rs_r[1, HALF - 1].astype(F32)
+                + far_r[...].astype(F32)
             )
 
     vr_copy(0, HALF).wait_recv()
@@ -479,7 +487,7 @@
     gy_copy(HALF, 0).wait_send()
     for s in range(1, HALF + 1):
         for way in range(2):
-            if s >= rs_first(way):
+            if s > 1:
                 rs_copy(way, s).wait_send()
             if s < HALF or way == 0:
                 vr_copy(way, s).wait_send()
@@ -517,8 +525,8 @@
         ((COLS, D), BF16),
         ((IMGS, D), BF16),
         ((COLS, IMGS), F32),
-        ((PIECE, IMGS), BF16),
-        ((2, TS, PIECE, IMGS), BF16),
+        ((PIECE, 2 * ROWS), BF16),
+        ((2, TS, PIECE, 2 * ROWS), BF16),
         ((E, IMGS), F32),
         ((E, IMGS), BF16),
         ((IMGS, E), BF16),
@@ -541,16 +549,18 @@
         ((2, HALF, TEXTS, E), BF16),
         ((HALF + 1, 2, TEXTS, E), BF16),
         ((HALF + 1, 2, TEXTS, E), BF16),
-        ((TS, PIECE, IMGS), BF16),
-        ((TS, PIECE, IMGS), BF16),
-        ((PIECE, IMGS), F32),
-        ((TS, PIECE, IMGS), BF16),
-        ((TS, PIECE, IMGS), BF16),
+        ((TEXTS, E), BF16),
+        ((TEXTS, E), BF16),
+        ((TS, PIECE, 2 * ROWS), BF16),
+        ((TS, PIECE, 2 * ROWS), BF16),
+        ((PIECE, 2 * ROWS), F32),
+        ((TS, PIECE, 2 * ROWS), BF16),
+        ((TS, PIECE, 2 * ROWS), BF16),
         ((WIDE, IMGS), F32),
         ((D, WIDE), F32),
-        ((2, HALF, ZROWS, WIDE), F32),
-        ((2, HALF, ZROWS, WIDE), F32),
-        ((4, ZROWS, WIDE), F32),
+        ((2, HALF, ZROWS, PIECE), F32),
+        ((2, HALF, ZROWS, PIECE), F32),
+        ((4, ZROWS, PIECE), F32),
     ]
     return pl.pallas_call(
         kernel,

time: 120 us -> 127 us (1.058)
  Pallas kernels: 116 us -> 123 us
    pallas_call x1, Pallas kernels: 116 us -> 123 us  [local(): pl.pallas_call(kernel, out_shape=(jax.ShapeDtypeStruct((TEXTS, E), F32),...]
where the time goes in v7:
time: 127 us
  Pallas kernels  123 us (97%)
  local copies, waits for them, and re-layouts  2.9 us (2%)
    pallas_call x1, Pallas kernels, local(): pl.pallas_call(kernel, out_shape=(jax.ShapeDtypeStruct((TEXTS, E), F32),...  123 us
    unnamed x2, local copies, waits for them, and re-layouts  2.9 us

profile of v7, /device:TPU:1, one launch (start us, length us, event | category | flops | bytes accessed | tf_op | source)
XLA Modules:
  0.0 126.6 jit_solution(1262367481502733503)
XLA Ops:
  0.6 123.0 %shard_map.95 = (f32[20,1152]{1,0:T(8,128)}, f32[18,144]{1,0:T(8,128)}) custom-call(bf16[160,1152]{1,0:T(8,128)(2,1)} %text_ref.1, f32[1152]{0:T(1024)} %ln_ref.1, bf16[538,1152]{1,0:T(8,128)(2,1)} %bitcast.2, bf16[538,1152]{1,0:T(8,128)(2,1)} %down_ref.1, f32[1152]{0:T(1024)} %fg_ref.1, bf16[144,1152]{1,0:T(8,128)(2,1)} %head_ref.1, ...), custom_call_target="tpu_custom_call" | custom-call | tf_op jit(solution)/shard_map/pallas_call | solution.py:565
  123.7 1.5 %copy.12 = f32[20,1152]{1,0:T(8,128)} copy(f32[20,1152]{1,0:T(8,128)} %get-tuple-element.4) | data formatting | bytes 184320
  125.2 1.3 %copy.13 = f32[18,144]{1,0:T(8,128)} copy(f32[18,144]{1,0:T(8,128)} %get-tuple-element.5) | data formatting | bytes 20736

commit v8 on v4

--- a/solution.py
+++ b/solution.py
@@ -22,7 +22,8 @@
 HALF = ZS // 2
 FF_DEV = 4304 // TS
 TEXTS = ROWS // TS
-CHUNK = 2 * TEXTS
+SLOT = 24
+CHUNK = 2 * SLOT
 IMGS = 384
 PIECE = E // (2 * TS)
 COLS = E // TS
@@ -178,7 +179,8 @@
     loads[L_DOWN].wait()
     mixed = mm(active, down_v[...])
     for j in range(TS):
-        mix_s[j] = mixed[TEXTS * j : TEXTS * (j + 1)].astype(BF16)
+        mix_s[j, 0:TEXTS] = mixed[TEXTS * j : TEXTS * (j + 1)].astype(BF16)
+        mix_s[j, TEXTS:SLOT] = jnp.zeros((SLOT - TEXTS, D), BF16)
 
     pl.semaphore_wait(barrier, len(greeted))
 
@@ -196,10 +198,11 @@
     loads[L_FEAT].wait()
     feat_copy = rcopy(feats.at[own_rows], feats.at[own_rows], S_FEAT, S_FEAT, c_peer)
     feat_copy.start()
-    mix_r[t] = jnp.zeros((TEXTS, D), BF16)
+    mix_r[t] = jnp.zeros((SLOT, D), BF16)
     with_hidden = mixed + hidden
     for j in range(TS):
-        mix_f[j] = with_hidden[TEXTS * j : TEXTS * (j + 1)]
+        mix_f[j, 0:TEXTS] = with_hidden[TEXTS * j : TEXTS * (j + 1)]
+        mix_f[j, TEXTS:SLOT] = jnp.zeros((SLOT - TEXTS, D), F32)
 
     loads[L_VIS].wait()
     feat_copy.wait_send()
@@ -216,20 +219,20 @@
         total = total + mix_r[j].astype(F32)
     normed = layer_norm(total, fg_ref[...].reshape(1, D)).astype(BF16).astype(F32)
     for j in range(TS):
-        nrm_s[j] = normed[:, COLS * j : COLS * (j + 1)].astype(BF16)
+        nrm_s[j, :, 0:COLS] = normed[:, COLS * j : COLS * (j + 1)].astype(BF16)
     exchange_start(nrm_s, nrm_r, S_NRM)
     nrm_r[t] = nrm_s[t]
 
     exchange_wait(nrm_s, nrm_r, S_NRM)
     for j in range(TS):
-        nrm_a[TEXTS * j : TEXTS * (j + 1), :] = nrm_r[j].astype(F32)
+        nrm_a[SLOT * j : SLOT * (j + 1), :] = nrm_r[j].astype(F32)[:, 0:COLS]
     loads[L_HEAD].wait()
     head_part = mm(nrm_a[...].astype(BF16), head_v[...])
     for j in range(TS):
-        head_f[j] = head_part[TEXTS * j : TEXTS * (j + 1)]
-        head_s[j] = head_part[TEXTS * j : TEXTS * (j + 1)].astype(BF16)
+        head_f[j] = head_part[SLOT * j : SLOT * (j + 1)]
+        head_s[j] = head_part[SLOT * j : SLOT * (j + 1)].astype(BF16)
     exchange_start(head_s, head_r, S_HEAD)
-    head_r[t] = jnp.zeros((TEXTS, E), BF16)
+    head_r[t] = jnp.zeros((SLOT, E), BF16)
 
     for k in range(1, TS):
         j = tpeer(k)
@@ -286,9 +289,9 @@
     pair_pieces = ((0, 0), (0, 1), (1, 0), (1, 1))
 
     def weigh(s, pieces):
-        rows = TEXTS * len(pieces)
+        rows = SLOT * len(pieces)
         for at, (way, half) in enumerate(pieces):
-            block_f[TEXTS * at : TEXTS * (at + 1), :] = texts[s, way, half].astype(F32)
+            block_f[SLOT * at : SLOT * (at + 1), :] = texts[s, way, half].astype(F32)
         block = block_f[0:rows, :].astype(BF16)
         dots = mm(block, img_ut[...])
         weights = jax.nn.sigmoid(logit_scale * dots + logit_bias)
@@ -310,7 +313,7 @@
     def text_terms(s, pieces, weights):
         terms = mm(weights, img_u[...])
         for at, (way, half) in enumerate(pieces):
-            part = terms[TEXTS * at : TEXTS * (at + 1)]
+            part = terms[SLOT * at : SLOT * (at + 1)]
             slot = way if pieces is pair_pieces else 0
             if half == 0:
                 grads[s, slot] = part
@@ -437,12 +440,13 @@
             gy_copy(0, 0).wait_recv()
             rs_copy(0, HALF).wait_recv()
             rs_copy(1, HALF).wait_recv()
-            tg_ref[...] = (
+            total_tg = (
                 grads[0, 0]
                 + gy_r[0, 0].astype(F32)
                 + rs_r[0, HALF - 1].astype(F32)
                 + rs_r[1, HALF - 1].astype(F32)
             )
+            tg_ref[...] = total_tg[0:TEXTS]
 
     vr_copy(0, HALF).wait_recv()
     vr_copy(1, HALF - 1).wait_recv()
@@ -524,23 +528,23 @@
         ((IMGS, E), BF16),
         ((1, IMGS), F32),
         ((1, IMGS), F32),
-        ((TS, TEXTS, D), BF16),
-        ((TS, TEXTS, D), F32),
-        ((TS, TEXTS, D), BF16),
-        ((TS, TEXTS, COLS), BF16),
-        ((TS, TEXTS, COLS), BF16),
-        ((ROWS, COLS), F32),
-        ((TS, TEXTS, E), BF16),
-        ((TS, TEXTS, E), F32),
-        ((TS, TEXTS, E), BF16),
+        ((TS, SLOT, D), BF16),
+        ((TS, SLOT, D), F32),
+        ((TS, SLOT, D), BF16),
+        ((TS, SLOT, 2 * WIDE), BF16),
+        ((TS, SLOT, 2 * WIDE), BF16),
+        ((TS * SLOT, COLS), F32),
+        ((TS, SLOT, E), BF16),
+        ((TS, SLOT, E), F32),
+        ((TS, SLOT, E), BF16),
         ((2 * CHUNK, E), F32),
-        ((HALF + 1, 2, 2, TEXTS, E), BF16),
-        ((HALF + 1, 2, TEXTS, E), F32),
+        ((HALF + 1, 2, 2, SLOT, E), BF16),
+        ((HALF + 1, 2, SLOT, E), F32),
         ((E, IMGS), F32),
-        ((2, HALF, TEXTS, E), BF16),
-        ((2, HALF, TEXTS, E), BF16),
-        ((HALF + 1, 2, TEXTS, E), BF16),
-        ((HALF + 1, 2, TEXTS, E), BF16),
+        ((2, HALF, SLOT, E), BF16),
+        ((2, HALF, SLOT, E), BF16),
+        ((HALF + 1, 2, SLOT, E), BF16),
+        ((HALF + 1, 2, SLOT, E), BF16),
         ((TS, PIECE, IMGS), BF16),
         ((TS, PIECE, IMGS), BF16),
         ((PIECE, IMGS), F32),

time: 120 us -> 120 us (level)
  no operation moved by 1% of the time
where the time goes in v8:
time: 120 us
  Pallas kernels  116 us (97%)
  local copies, waits for them, and re-layouts  2.9 us (2%)
    pallas_call x1, Pallas kernels, local(): pl.pallas_call(kernel, out_shape=(jax.ShapeDtypeStruct((TEXTS, E), F32),...  116 us
    unnamed x2, local copies, waits for them, and re-layouts  2.9 us

profile of v8, /device:TPU:1, one launch (start us, length us, event | category | flops | bytes accessed | tf_op | source)
XLA Modules:
  0.0 119.5 jit_solution(13757166693212464617)
XLA Ops:
  0.6 116.0 %shard_map.95 = (f32[20,1152]{1,0:T(8,128)}, f32[18,144]{1,0:T(8,128)}) custom-call(bf16[160,1152]{1,0:T(8,128)(2,1)} %text_ref.1, f32[1152]{0:T(1024)} %ln_ref.1, bf16[538,1152]{1,0:T(8,128)(2,1)} %bitcast.2, bf16[538,1152]{1,0:T(8,128)(2,1)} %down_ref.1, f32[1152]{0:T(1024)} %fg_ref.1, bf16[144,1152]{1,0:T(8,128)(2,1)} %head_ref.1, ...), custom_call_target="tpu_custom_call" | custom-call | tf_op jit(solution)/shard_map/pallas_call | solution.py:559
  116.7 1.5 %copy.12 = f32[20,1152]{1,0:T(8,128)} copy(f32[20,1152]{1,0:T(8,128)} %get-tuple-element.4) | data formatting | bytes 184320
  118.2 1.3 %copy.13 = f32[18,144]{1,0:T(8,128)} copy(f32[18,144]{1,0:T(8,128)} %get-tuple-element.5) | data formatting | bytes 20736

commit v9 on v8

--- a/solution.py
+++ b/solution.py
@@ -372,7 +372,7 @@
 
     ag_copy(HALF, 0, 0).wait_recv()
     ag_copy(HALF, 1, 1).wait_recv()
-    text_terms(HALF, far_pieces, weigh(HALF, far_pieces))
+    far_weights = weigh(HALF, far_pieces)
 
     radial = rad_ref[...]
     inverse = inv_ref[...]
@@ -388,8 +388,9 @@
     for k in range(1, TS + 1):
         cx_s[tpeer(k)] = emb_piece(tpeer(k), 1 - c).astype(BF16)
         cx_copy(k).start()
+    text_terms(HALF, far_pieces, far_weights)
+    rs_step(1, 2)
     rs_step(0, 1)
-    rs_step(1, 2)
     for k in range(1, TS + 1):
         j = tpeer(k)
         value = emb_piece(j, c)
@@ -424,8 +425,8 @@
         value = vg_chunk(owner)
         if s > 1:
             vr_copy(way, s - 1).wait_recv()
-            value = value + vr_r[way, s - 2]
-        vr_s[way, s - 1] = value
+            value = value + vr_r[way, s - 2].astype(F32)
+        vr_s[way, s - 1] = value.astype(BF16)
         vr_copy(way, s).start()
 
     for s in range(1, HALF + 1):
@@ -450,7 +451,7 @@
 
     vr_copy(0, HALF).wait_recv()
     vr_copy(1, HALF - 1).wait_recv()
-    fx[q] = vg_chunk(z) + vr_r[0, HALF - 1] + vr_r[1, HALF - 2]
+    fx[q] = vg_chunk(z) + vr_r[0, HALF - 1].astype(F32) + vr_r[1, HALF - 2].astype(F32)
     for k in range(1, 4):
         rcopy(fx.at[q], fx.at[q], S_FX + k, S_FX + q, fx_peers[k - 1]).start()
 
@@ -552,8 +553,8 @@
         ((TS, PIECE, IMGS), BF16),
         ((WIDE, IMGS), F32),
         ((D, WIDE), F32),
-        ((2, HALF, ZROWS, WIDE), F32),
-        ((2, HALF, ZROWS, WIDE), F32),
+        ((2, HALF, ZROWS, WIDE), BF16),
+        ((2, HALF, ZROWS, WIDE), BF16),
         ((4, ZROWS, WIDE), F32),
     ]
     return pl.pallas_call(

time: 120 us -> 120 us (level)
  no operation moved by 1% of the time
where the time goes in v9:
time: 120 us
  Pallas kernels  116 us (97%)
  local copies, waits for them, and re-layouts  2.9 us (2%)
    pallas_call x1, Pallas kernels, local(): pl.pallas_call(kernel, out_shape=(jax.ShapeDtypeStruct((TEXTS, E), F32),...  116 us
    unnamed x2, local copies, waits for them, and re-layouts  2.9 us

profile of v9, /device:TPU:1, one launch (start us, length us, event | category | flops | bytes accessed | tf_op | source)
XLA Modules:
  0.0 119.7 jit_solution(11067335350375868500)
XLA Ops:
  0.6 116.2 %shard_map.95 = (f32[20,1152]{1,0:T(8,128)}, f32[18,144]{1,0:T(8,128)}) custom-call(bf16[160,1152]{1,0:T(8,128)(2,1)} %text_ref.1, f32[1152]{0:T(1024)} %ln_ref.1, bf16[538,1152]{1,0:T(8,128)(2,1)} %bitcast.2, bf16[538,1152]{1,0:T(8,128)(2,1)} %down_ref.1, f32[1152]{0:T(1024)} %fg_ref.1, bf16[144,1152]{1,0:T(8,128)(2,1)} %head_ref.1, ...), custom_call_target="tpu_custom_call" | custom-call | tf_op jit(solution)/shard_map/pallas_call | solution.py:560
  116.8 1.5 %copy.12 = f32[20,1152]{1,0:T(8,128)} copy(f32[20,1152]{1,0:T(8,128)} %get-tuple-element.4) | data formatting | bytes 184320
  118.4 1.3 %copy.13 = f32[18,144]{1,0:T(8,128)} copy(f32[18,144]{1,0:T(8,128)} %get-tuple-element.5) | data formatting | bytes 20736

commit v10 on v8

--- a/solution.py
+++ b/solution.py
@@ -55,7 +55,8 @@
 S_AG = S_YH + 1
 S_RS = S_AG + 4 * HALF
 S_GY = S_RS + 2 * HALF
-S_CX = S_GY + 2 * HALF + 2
+S_FAR = S_GY + 2 * HALF + 2
+S_CX = S_FAR + 1
 S_PX = S_CX + TS
 S_VRP = S_PX + TS
 S_VRM = S_VRP + HALF
@@ -105,6 +106,8 @@
     rs_r,
     gy_s,
     gy_r,
+    far_s,
+    far_r,
     cx_s,
     cx_r,
     px_f,
@@ -148,7 +151,8 @@
         )
 
     barrier = pltpu.get_barrier_semaphore()
-    greeted = [z_next, z_prev] + [(d, tpeer(k)) for k in range(1, TS)]
+    z_far = (lax.rem(z + HALF, ZS) * 4 + base, t)
+    greeted = [z_next, z_prev, z_far] + [(d, tpeer(k)) for k in range(1, TS)]
     fx_peers = [(4 * z + lax.rem(q + k, 4), t) for k in range(1, 4)]
     greeted = greeted + fx_peers
     for dev in greeted:
@@ -356,23 +360,23 @@
         sem = S_RS + 2 * (s - 1) + way
         return rcopy(rs_s.at[way, s - 1], rs_r.at[way, s - 1], sem, sem, (z_next, z_prev)[way])
 
-    def rs_first(way):
-        return 1 + way
-
-    def rs_step(way, s):
+    def rs_step(s):
         left = HALF + 1 - s
-        slot = 0 if s == 1 else 1 - way
-        gy_copy(left, slot).wait_recv()
-        value = grads[left, slot] + gy_r[left, slot].astype(F32)
-        if s > rs_first(way):
-            rs_copy(way, s - 1).wait_recv()
-            value = value + rs_r[way, s - 2].astype(F32)
-        rs_s[way, s - 1] = value.astype(BF16)
-        rs_copy(way, s).start()
+        for way in range(2):
+            slot = 1 - way
+            gy_copy(left, slot).wait_recv()
+            value = grads[left, slot] + gy_r[left, slot].astype(F32)
+            if s > 2:
+                rs_copy(way, s - 1).wait_recv()
+                value = value + rs_r[way, s - 2].astype(F32)
+            rs_s[way, s - 1] = value.astype(BF16)
+            rs_copy(way, s).start()
+
+    far_copy = rcopy(far_s, far_r, S_FAR, S_FAR, z_far)
 
     ag_copy(HALF, 0, 0).wait_recv()
     ag_copy(HALF, 1, 1).wait_recv()
-    text_terms(HALF, far_pieces, weigh(HALF, far_pieces))
+    far_weights = weigh(HALF, far_pieces)
 
     radial = rad_ref[...]
     inverse = inv_ref[...]
@@ -388,8 +392,8 @@
     for k in range(1, TS + 1):
         cx_s[tpeer(k)] = emb_piece(tpeer(k), 1 - c).astype(BF16)
         cx_copy(k).start()
-    rs_step(0, 1)
-    rs_step(1, 2)
+    rs_step(2)
+    text_terms(HALF, far_pieces, far_weights)
     for k in range(1, TS + 1):
         j = tpeer(k)
         value = emb_piece(j, c)
@@ -402,9 +406,11 @@
             px_f[...] = value
     px_r[t] = jnp.zeros((PIECE, IMGS), BF16)
     emb_b[PIECE:WIDE, :] = jnp.zeros((WIDE - PIECE, IMGS), F32)
-    for s in range(2, 4):
-        rs_step(0, s)
-        rs_step(1, s + 1)
+    rs_step(3)
+    gy_copy(HALF, 0).wait_recv()
+    far_s[...] = (grads[HALF, 0] + gy_r[HALF, 0].astype(F32)).astype(BF16)
+    far_copy.start()
+    rs_step(4)
     exchange_wait(px_s, px_r, S_PX)
     emb_grad = px_f[...]
     for j in range(TS):
@@ -432,11 +438,10 @@
         vr_step(0, s)
         if s < HALF:
             vr_step(1, s)
-        if s + 3 <= HALF:
-            rs_step(0, s + 3)
         if s + 4 <= HALF:
-            rs_step(1, s + 4)
-        if s == HALF - 2:
+            rs_step(s + 4)
+        if s == HALF - 3:
+            far_copy.wait()
             gy_copy(0, 0).wait_recv()
             rs_copy(0, HALF).wait_recv()
             rs_copy(1, HALF).wait_recv()
@@ -445,6 +450,7 @@
                 + gy_r[0, 0].astype(F32)
                 + rs_r[0, HALF - 1].astype(F32)
                 + rs_r[1, HALF - 1].astype(F32)
+                + far_r[...].astype(F32)
             )
             tg_ref[...] = total_tg[0:TEXTS]
 
@@ -483,7 +489,7 @@
     gy_copy(HALF, 0).wait_send()
     for s in range(1, HALF + 1):
         for way in range(2):
-            if s >= rs_first(way):
+            if s > 1:
                 rs_copy(way, s).wait_send()
             if s < HALF or way == 0:
                 vr_copy(way, s).wait_send()
@@ -545,6 +551,8 @@
         ((2, HALF, SLOT, E), BF16),
         ((HALF + 1, 2, SLOT, E), BF16),
         ((HALF + 1, 2, SLOT, E), BF16),
+        ((SLOT, E), BF16),
+        ((SLOT, E), BF16),
         ((TS, PIECE, IMGS), BF16),
         ((TS, PIECE, IMGS), BF16),
         ((PIECE, IMGS), F32),

time: 120 us -> 123 us (1.025)
  Pallas kernels: 116 us -> 119 us
    pallas_call x1, Pallas kernels: 116 us -> 119 us  [local(): pl.pallas_call(kernel, out_shape=(jax.ShapeDtypeStruct((TEXTS, E), F32),...]
where the time goes in v10:
time: 123 us
  Pallas kernels  119 us (97%)
  local copies, waits for them, and re-layouts  2.9 us (2%)
    pallas_call x1, Pallas kernels, local(): pl.pallas_call(kernel, out_shape=(jax.ShapeDtypeStruct((TEXTS, E), F32),...  119 us
    unnamed x2, local copies, waits for them, and re-layouts  2.9 us

profile of v10, /device:TPU:1, one launch (start us, length us, event | category | flops | bytes accessed | tf_op | source)
XLA Modules:
  0.0 122.7 jit_solution(5757285902251275210)
XLA Ops:
  0.6 119.1 %shard_map.95 = (f32[20,1152]{1,0:T(8,128)}, f32[18,144]{1,0:T(8,128)}) custom-call(bf16[160,1152]{1,0:T(8,128)(2,1)} %text_ref.1, f32[1152]{0:T(1024)} %ln_ref.1, bf16[538,1152]{1,0:T(8,128)(2,1)} %bitcast.2, bf16[538,1152]{1,0:T(8,128)(2,1)} %down_ref.1, f32[1152]{0:T(1024)} %fg_ref.1, bf16[144,1152]{1,0:T(8,128)(2,1)} %head_ref.1, ...), custom_call_target="tpu_custom_call" | custom-call | tf_op jit(solution)/shard_map/pallas_call | solution.py:567
  119.8 1.5 %copy.12 = f32[20,1152]{1,0:T(8,128)} copy(f32[20,1152]{1,0:T(8,128)} %get-tuple-element.4) | data formatting | bytes 184320
  121.3 1.3 %copy.13 = f32[18,144]{1,0:T(8,128)} copy(f32[18,144]{1,0:T(8,128)} %get-tuple-element.5) | data formatting | bytes 20736
